TPU v7x, 128 devices: a whole 4x4x4 slice. The times are simulated.
128 devices in a mesh: kvh: 8 (over y, core), split: 16 (over z, x).
Axes of the slice: x: 4, y: 4, z: 4, core: 2. Of those that a mesh axis runs over, the one named last changes fastest.
Arguments:
- queries: bfloat16 [8, 64, 64, 128], P('kvh', 'split'), may hold values from -600 to 600, as said below
- tree_keys: bfloat16 [8, 64, 8, 128], P('kvh', 'split'), may hold values from -16 to 16
- tree_values: bfloat16 [8, 64, 8, 128], P('kvh', 'split'), may hold values from -6 to 6
- key_cache: bfloat16 [8, 3072, 128, 128], P('kvh', 'split'), may hold values from -6 to 6
- value_cache: bfloat16 [8, 3072, 128, 128], P('kvh', 'split'), may hold values from -6 to 6
- page_request: int32 [3072], P('split'), may hold values from 0 to 7, as said below
- page_index: int32 [3072], P('split'), may hold values from 0 to 383, as said below
- ctx_len: int32 [8], replicated, may hold values from 24576 to 49152, as said below
- tree_len: int32 [8], replicated, may hold values from 16 to 64, as said below
- tree_mask: int32 [8, 64, 64], replicated, may hold values from 0 to 1, as said below
Outputs:
- attended: bfloat16 [8, 64, 64, 128], P('kvh', 'split')
Inputs may be any that keep to these rules, and one draw needn't show every extreme that they name: `page_request`: each request owns exactly 384 physical pages, spread over the devices in an order drawn from the seed. `page_index`: within one request every place 0 to 383 appears once. `ctx_len`: some request has exactly 49152 cached tokens. `tree_len`: some request has exactly 64 draft tokens. `tree_mask`: row i holds 1 at i and at the ancestors of draft token i in its tree, whose parents come earlier; 0 elsewhere. `queries`: query entries.
All inputs are finite; a program needn't handle non-finite values.
Results may differ from a plain program's by a relative error of at most 0.0085.
Values may be sent and summed in bfloat16 or wider, within the bound.
No kernel may reach another device: no remote copies, remote signals or barrier semaphores. Data moves between devices by JAX's collectives and lax.ppermute only.
A program may use at most 128 MiB of HBM per device.

v0:
```python
import jax
import jax.numpy as jnp
from jax import lax
from jax.sharding import PartitionSpec as P

BLK = 8


def joined(value, axis, combine):
    everything = jax.tree.map(lambda part: lax.all_gather(part, axis), value)
    first = jax.tree.map(lambda part: part[0], everything)

    def hop(k, so_far):
        return combine(so_far, jax.tree.map(lambda part: part[k], everything))

    return lax.fori_loop(1, lax.axis_size(axis), hop, first)


def cache_block(carry, item, q_rows, ctx_len):
    run_max, run_sum, running_output = carry
    key_rows, value_rows, owner, index = item
    requests = q_rows.shape[0]
    page = key_rows.shape[1]
    score_scale = key_rows.shape[2] ** (-0.5)
    selected_rows = jnp.take(q_rows, owner, axis=0)
    logit_scores = (
        jnp.einsum("zal,zel->zae", selected_rows, key_rows, preferred_element_type=jnp.float32)
        * score_scale
    )
    limit = jnp.take(ctx_len, owner)
    position = index[:, None] * page + jnp.arange(page, dtype=jnp.int32)[None, :]
    valid = (position < limit[:, None])[:, None, :]
    masked = jnp.where(valid, logit_scores, -1e30)
    page_max = masked.max(axis=2)
    member = owner[:, None] == jnp.arange(requests, dtype=jnp.int32)[None, :]
    block_max = jnp.where(member[:, :, None], page_max[:, None, :], -1e30).max(axis=0)
    new_max = jnp.maximum(run_max, block_max)
    shift = jnp.take(new_max, owner, axis=0)
    prob_weights = jnp.where(valid, jnp.exp(masked - shift[:, :, None]), 0.0).astype(jnp.bfloat16)
    partial_output = jnp.einsum(
        "upl,ulz->upz", prob_weights, value_rows, preferred_element_type=jnp.float32
    )
    part_sum = prob_weights.astype(jnp.float32).sum(axis=2)
    one_hot_select = member.astype(jnp.float32)
    rescale_factor = jnp.exp(run_max - new_max)
    run_sum = run_sum * rescale_factor + jnp.einsum(
        "br,bq->rq", one_hot_select, part_sum, precision=lax.Precision.HIGHEST
    )
    running_output = running_output * rescale_factor[:, :, None] + jnp.einsum(
        "ht,hcg->tcg", one_hot_select, partial_output, precision=lax.Precision.HIGHEST
    )
    return ((new_max, run_sum, running_output), None)


def join_partials(first, second):
    max_one, sum_one, acc_one = first
    max_two, sum_two, acc_two = second
    top = jnp.maximum(max_one, max_two)
    f_one = jnp.exp(max_one - top)
    f_two = jnp.exp(max_two - top)
    return (
        top,
        sum_one * f_one + sum_two * f_two,
        acc_one * f_one[..., None] + acc_two * f_two[..., None],
    )


def per_device(
    queries,
    tree_keys,
    tree_values,
    key_cache,
    value_cache,
    page_request,
    page_index,
    ctx_len,
    tree_len,
    tree_mask,
):
    q_own, tk_own, tv_own = (
        lax.all_to_all(queries, "kvh", split_axis=2, concat_axis=0, tiled=True),
        lax.all_to_all(tree_keys, "kvh", split_axis=2, concat_axis=0, tiled=True),
        lax.all_to_all(tree_values, "kvh", split_axis=2, concat_axis=0, tiled=True),
    )
    requests, tl, group, hdim = q_own.shape
    all_q, all_tk, all_tv = (
        lax.all_gather(q_own, "split", axis=1, tiled=True),
        lax.all_gather(tk_own, "split", axis=1, tiled=True),
        lax.all_gather(tv_own, "split", axis=1, tiled=True),
    )
    tree = all_q.shape[1]
    rows = tree * group
    q_rows = all_q.reshape(requests, rows, hdim)
    pages = key_cache.shape[1]
    page = key_cache.shape[2]
    blocks = pages // BLK
    items = (
        key_cache.reshape(blocks, BLK, page, hdim),
        value_cache.reshape(blocks, BLK, page, hdim),
        page_request.reshape(blocks, BLK),
        page_index.reshape(blocks, BLK),
    )
    start_state = (
        jnp.full((requests, rows), -1e30, jnp.float32),
        jnp.zeros((requests, rows), jnp.float32),
        jnp.zeros((requests, rows, hdim), jnp.float32),
    )
    (cmax, csum, cacc), unused = lax.scan(
        lambda c, it: cache_block(c, it, q_rows, ctx_len), start_state, items
    )
    cmax = cmax.reshape(requests, tree, group)
    csum = csum.reshape(requests, tree, group)
    cacc = cacc.reshape(requests, tree, group, hdim)
    first_row = lax.axis_index("split") * tl
    gmax, gsum, gacc = joined((cmax, csum, cacc), "split", join_partials)
    gmax = lax.dynamic_slice_in_dim(gmax, first_row, tl, 1)
    gsum = lax.dynamic_slice_in_dim(gsum, first_row, tl, 1)
    gacc = lax.dynamic_slice_in_dim(gacc, first_row, tl, 1)
    tk = all_tk[:, :, 0, :]
    tv = all_tv[:, :, 0, :]
    tscores = jnp.einsum(
        "riqd,rkd->riqk", q_own, tk, preferred_element_type=jnp.float32
    ) * hdim ** (-0.5)
    mask_rows = lax.dynamic_slice_in_dim(tree_mask, first_row, tl, 1)
    allowed = (mask_rows == 1)[:, :, None, :]
    tmasked = jnp.where(allowed, tscores, -1e30)
    peak = jnp.maximum(gmax, tmasked.max(axis=3))
    tweights = jnp.where(allowed, jnp.exp(tmasked - peak[..., None]), 0.0).astype(jnp.bfloat16)
    rescale_factor = jnp.exp(gmax - peak)
    total = gsum * rescale_factor + tweights.astype(jnp.float32).sum(axis=3)
    numer = gacc * rescale_factor[..., None] + jnp.einsum(
        "riqk,rkd->riqd", tweights, tv, preferred_element_type=jnp.float32
    )
    slots = first_row + jnp.arange(tl, dtype=jnp.int32)
    live = (slots[None, :] < tree_len[:, None])[:, :, None, None]
    result = jnp.where(live, numer / total[..., None], 0.0).astype(jnp.bfloat16)
    return lax.all_to_all(result, "kvh", split_axis=0, concat_axis=2, tiled=True)


def solution(mesh):
    in_specs = (
        P("kvh", "split", None, None),
        P("kvh", "split", None, None),
        P("kvh", "split", None, None),
        P("kvh", "split", None, None),
        P("kvh", "split", None, None),
        P("split"),
        P("split"),
        P(),
        P(),
        P(),
    )
    out_specs = P("kvh", "split", None, None)
    return jax.shard_map(
        per_device, mesh=mesh, in_specs=in_specs, out_specs=out_specs, check_vma=False
    )
```

profile of v0, /device:TPU:1, one launch (start us, length us, event | category | flops | bytes accessed | tf_op | source)
XLA Modules:
  0.0 728.5 jit_solution(9946699748682930684)
XLA Ops:
  7.4 10.6 %all_to_all.72 = bf16[1,4,64,128]{3,1,0,2:T(4,128)(2,1)S(1)} all-to-all(bf16[1,4,64,128]{3,1,0,2:T(4,128)(2,1)S(1)} %copy.66), channel_id=1, replica_groups=mesh['kvh'=8,'split'=16] {'kvh'}, dimensions={2} | all-to-all | bytes 131072 | tf_op jit(solution)/shard_map/all_to_all | solution.py:81
  20.3 41.1 %all-gather.8.cloned.1.call-done = bf16[8,1,64,8,128]{4,3,2,0,1:T(8,128)(2,1)} async-done(((bf16[8,1,4,8,128]{4,3,2,0,1:T(8,128)(2,1)}), bf16[8,1,64,8,128]{4,3,2,0,1:T(8,128)(2,1)}) %all-gather.8.cloned.1.call-update) | async-done | bytes 1048592 | tf_op jit(solution)/shard_map/all_gather | solution.py:87
  61.4 383.5 %while.35 = (s32[]{:T(128)}, f32[8,512]{1,0:T(8,128)S(1)}, f32[8,512]{1,0:T(8,128)S(1)}, f32[8,512,128]{2,0,1:T(8,128)}, s32[24,8]{1,0:T(8,128)S(1)}, /*index=5*...) while((s32[]{:T(128)}, f32[8,512]{1,0:T(8,128)S(1)}, ...), condition=%wide.region_4.5_spmd.clone, body=%wide.region_0.4_spmd.clone.sunk | while | flops 329207072 | bytes 18704388 | solution.py:108
  85.9 6.1 fusion.64
  101.9 6.1 fusion.64
  117.9 6.1 fusion.64
  133.9 6.1 fusion.64
  149.9 6.1 fusion.64
  165.9 6.1 fusion.64
  181.9 6.1 fusion.64
  198.0 6.1 fusion.64
  214.0 6.1 fusion.64
  230.0 6.1 fusion.64
  246.0 6.1 fusion.64
  262.0 6.1 fusion.64
  278.0 6.1 fusion.64
  294.0 6.1 fusion.64
  310.0 6.1 fusion.64
  326.0 6.1 fusion.64
  358.0 6.1 fusion.64
  374.0 6.1 fusion.64
  406.0 6.1 fusion.64
  422.0 6.1 fusion.64
  438.0 6.1 fusion.64
  449.6 6.3 all-to-all-start.1
  469.2 19.8 %all-gather.1 = bf16[8,1,64,1,128]{4,0,3,1,2:T(8,128)(2,1)S(1)} all-gather(bf16[8,1,4,1,128]{4,0,3,1,2:T(8,128)(2,1)S(1)} %copy.74), channel_id=3, replica_groups=mesh['kvh'=8,'split'=16] {'split'}, dimensions={2}, use_global_device_ids=true | all-gather | bytes 139264 | tf_op jit(solution)/shard_map/all_gather | solution.py:88
  489.0 16.9 %all-gather.2 = bf16[8,1,64,1,128]{4,0,3,1,2:T(8,128)(2,1)S(1)} all-gather(bf16[8,1,4,1,128]{4,0,3,1,2:T(8,128)(2,1)S(1)} %copy.77), channel_id=4, replica_groups=mesh['kvh'=8,'split'=16] {'split'}, dimensions={2}, use_global_device_ids=true | all-gather | bytes 139264 | tf_op jit(solution)/shard_map/all_gather | solution.py:89
  506.8 21.5 %all_gather.20 = f32[16,8,64,8]{2,3,1,0:T(8,128)S(1)} all-gather(f32[1,8,64,8]{2,3,1,0:T(8,128)S(1)} %copy.70), channel_id=1, replica_groups=mesh['kvh'=8,'split'=16] {'split'}, dimensions={0}, use_global_device_ids=true | all-gather | bytes 278528 | tf_op jit(solution)/shard_map/all_gather | solution.py:10
  528.3 21.2 %all_gather.19 = f32[16,8,64,8]{2,3,1,0:T(8,128)} all-gather(f32[1,8,64,8]{2,3,1,0:T(8,128)S(1)} %copy.69), channel_id=1, replica_groups=mesh['kvh'=8,'split'=16] {'split'}, dimensions={0}, use_global_device_ids=true | all-gather | bytes 278528 | tf_op jit(solution)/shard_map/all_gather | solution.py:10
  550.3 102.2 %all-gather.6.cloned.1.call-done = f32[16,8,64,8,128]{4,3,2,1,0:T(8,128)} async-done(((f32[1,8,64,8,128]{4,3,2,1,0:T(8,128)}), f32[16,8,64,8,128]{4,3,2,1,0:T(8,128)}) %all-gather.6.cloned.1.call-update) | async-done | bytes 33554448 | tf_op jit(solution)/shard_map/all_gather | solution.py:10
  654.2 56.5 %while.34 = (s32[]{:T(128)}, f32[8,64,8]{1,2,0:T(8,128)S(1)}, f32[8,64,8]{1,2,0:T(8,128)S(1)}, f32[8,64,8,128]{3,2,1,0:T(8,128)S(1)}, f32[16,8,64,8]{2,3,1,0:T(8...) while((s32[]{:T(128)}, f32[8,64,8]{1,2,0:T(8,128)S(1)}, ...), condition=%wide.region_6.7_spmd, body=%wide.region_5.6_spmd.sunk | while | flops 1597445 | bytes 6520983 | solution.py:16
  711.5 9.5 %all_to_all.73 = bf16[8,4,8,128]{3,2,1,0:T(8,128)(2,1)S(1)} all-to-all(bf16[8,4,8,128]{3,2,1,0:T(8,128)(2,1)S(1)} %fusion.31), channel_id=1, replica_groups=mesh['kvh'=8,'split'=16] {'kvh'}, dimensions={0} | all-to-all | bytes 131072 | tf_op jit(solution)/shard_map/all_to_all | solution.py:137
  (538 shorter events, 334.8 us)
Async XLA Ops:
  6.5 54.9 %all-gather.8.cloned.1.call-start = ((), (), s32[]{:S(2)}) async-start(), calls=%async_computation.5 | async-start | bytes 1114112 | tf_op jit(solution)/shard_map/all_gather | solution.py:87
  18.7 633.7 %all-gather.6.cloned.1.call-start = ((), (), s32[]{:S(2)}) async-start(), calls=%async_computation.4 | async-start | bytes 35651584 | tf_op jit(solution)/shard_map/all_gather | solution.py:10
  448.3 0.7 copy-start
  448.3 7.6 %copy-start.2 = (s32[8]{0:T(128)S(1)}, s32[8]{0:T(128)}, u32[]{:S(2)}) copy-start(s32[8]{0:T(128)} %param.22) | copy-start | bytes 100
  448.3 7.7 %copy-start.1 = (bf16[1,4,8,128]{3,2,1,0:T(8,128)(2,1)S(1)}, bf16[1,4,8,128]{3,2,1,0:T(8,128)(2,1)}, u32[]{:S(2)}) copy-start(bf16[1,4,8,128]{3,2,1,0:T(8,128)(2,1)} %param.16) | copy-start | bytes 24580
  449.6 10.9 %all-to-all-start.1 = ((bf16[1,4,8,128]{3,1,0,2:T(4,128)(2,1)}), bf16[1,4,8,128]{3,1,0,2:T(4,128)(2,1)S(1)}, u32[]{:S(2)}, u32[]{:S(2)}) async-start(bf16[1,4,8,128]{3,1,0,2:T(4,128)(2,1)} %copy.73), calls=%async_computation.1 | async-start | bytes 16384 | tf_op jit(solution)/shard_map/all_to_all | solution.py:82
  460.5 8.7 %all-to-all-start.2 = ((bf16[1,4,8,128]{3,1,0,2:T(4,128)(2,1)}), bf16[1,4,8,128]{3,1,0,2:T(4,128)(2,1)S(1)}, u32[]{:S(2)}, u32[]{:S(2)}) async-start(bf16[1,4,8,128]{3,1,0,2:T(4,128)(2,1)} %copy.76), calls=%async_computation.2 | async-start | bytes 16384 | tf_op jit(solution)/shard_map/all_to_all | solution.py:83
Sparse Core Ops, SparseCore 0:
  18.8 42.5 all-gather.7
  448.4 203.9 all-gather.5
where the time goes:
time: 733 us; the launch traced here: 728 us
  matrix products  262 us (36%)
  waiting for transfers between devices  151 us (21%)
  local copies, waits for them, and re-layouts  113 us (15%)
  blocking collectives  99.6 us (14%)
  other arithmetic  75.8 us (10%)
  between operations  13.5 us (2%)
  starting transfers between devices  10.3 us (1%)
    dot_general x24, matrix products, cache_block(): jnp.einsum('ht,hcg->tcg', one_hot_select, partial_output, precision=lax.P...  146 us
    all_gather x1, waiting for transfers between devices, joined(): everything = jax.tree.map(lambda part: lax.all_gather(part, axis), value)  102 us
    dot_general x24, matrix products, cache_block(): jnp.einsum('upl,ulz->upz', prob_weights, value_rows, preferred_element_ty...  76.6 us
    gather x24, local copies, waits for them, and re-layouts, cache_block(): selected_rows = jnp.take(q_rows, owner, axis=0)  47.4 us
    all_gather x2, blocking collectives, joined(): everything = jax.tree.map(lambda part: lax.all_gather(part, axis), value)  42.7 us
    all_gather x1, waiting for transfers between devices, per_device(): lax.all_gather(q_own, 'split', axis=1, tiled=True)  41.1 us
    add x15, other arithmetic, join_partials(): acc_one * f_one[..., None] + acc_two * f_two[..., None]  40.1 us
    dot_general x24, matrix products, cache_block(): jnp.einsum('zal,zel->zae', selected_rows, key_rows, preferred_element_typ...  36.4 us
  transfers between devices with their start and end apart: 4, of which 4 were waited for; matrix products, arithmetic and copies ran while one was open for 1% of the time, Pallas kernels for 0%

commit v1 on v0

v1 whole, which is shorter than its diff:
```python
import functools

import jax
import jax.numpy as jnp
from jax import lax
from jax.experimental import pallas as pl
from jax.experimental.pallas import tpu as pltpu
from jax.sharding import PartitionSpec as P

BOTH = ("kvh", "split")
NEG = -1e30
LOG2E = 1.4426950408889634
HUGE = 2.0**100
CHUNK = 128
SLOTS = 256
F32 = jnp.float32
BF16 = jnp.bfloat16

NT = (((1,), (1,)), ((), ()))


def column_bias(lims, page):
    col = lax.broadcasted_iota(jnp.int32, (1, page), 1)
    return jnp.concatenate([jnp.where(col < x, 0.0, NEG) for x in lims], 1)


def attn_kernel(
    dims,
    meta,
    x_ref,
    mask_ref,
    k_ref,
    v_ref,
    o_ref,
    m_s,
    l_s,
    acc,
    top,
    plist,
    plim,
    cnt,
):
    requests, splits, tl, group, pages, page, hd = dims
    rows = tl * group
    full_rows = splits * rows
    scale = hd**-0.5 * LOG2E
    i_ctx, i_tl, i_me = 2 * pages, 2 * pages + requests, 2 * pages + 2 * requests

    for r in range(requests):
        cnt[r] = 0

    def scan(p, carry):
        r = meta[p]
        lim = meta[i_ctx + r] - meta[pages + p] * page
        c = cnt[r]
        plist[r * SLOTS + c] = p
        plim[r * SLOTS + c] = lim
        cnt[r] = jnp.where(lim > 0, c + 1, c)
        return carry

    lax.fori_loop(0, pages, scan, 0)

    me = meta[i_me]
    per = splits // requests
    tree_request = me // per
    part = me % per
    tree_rows = full_rows // per
    top[...] = jnp.zeros_like(top)

    def queries(r, count):
        blocks = count // rows
        return x_ref[pl.ds(r * splits, blocks), 0:rows, :].reshape(count, hd)

    def tree_page():
        first = pl.multiple_of(part * tree_rows, tree_rows)
        blk = tree_rows // rows
        q = x_ref[pl.ds(tree_request * splits + part * blk, blk), 0:rows, :]
        kv = x_ref[pl.ds(tree_request * splits, splits), rows : rows + 2 * tl, :]
        kv = kv.reshape(splits * 2 * tl, hd)
        wide = splits * 2 * tl
        values = pltpu.roll(kv.astype(F32), wide - tl, 0).astype(BF16)
        drafts = tree_rows // group
        mask = mask_ref[tree_request, pl.ds(part * drafts, drafts), :]
        tree = mask.shape[1]
        src = lax.broadcasted_iota(jnp.int32, (tree, wide), 0)
        dst = lax.broadcasted_iota(jnp.int32, (tree, wide), 1)
        pick = (src // tl == dst // (2 * tl)) & (src % tl == dst % (2 * tl))
        seen = jnp.dot(
            (mask == 1).astype(F32).astype(BF16),
            pick.astype(F32).astype(BF16),
            preferred_element_type=F32,
        )
        bias = jnp.where(seen > 0.5, 0.0, NEG)
        bias = jnp.broadcast_to(bias[:, None, :], (drafts, group, wide))
        s = lax.dot_general(q.reshape(tree_rows, hd), kv, NT, preferred_element_type=F32)
        return first, s + bias.reshape(tree_rows, wide), values

    def block_of(r, n, start, nb):
        ids, lims = [], []
        for j in range(nb):
            there = start + j < n
            at = r * SLOTS + jnp.minimum(start + j, n)
            ids.append(jnp.where(there, plist[at], 0))
            lims.append(jnp.where(there, plim[at], 0))
        k = jnp.concatenate([k_ref[0, i] for i in ids], 0)
        v = jnp.concatenate([v_ref[0, i] for i in ids], 0)
        return k, v, column_bias(lims, page)

    def add(at, s, v):
        m = m_s[at, :]
        ps = [
            jnp.exp2(s[:, j : j + page] * scale - m) for j in range(0, s.shape[1], page)
        ]
        l_s[at, :] += functools.reduce(jnp.add, ps)
        p = jnp.concatenate([x.astype(BF16) for x in ps], 1)
        acc[at, :] += jnp.dot(p, v, preferred_element_type=F32)

    def add_online(at, s, v):
        old = m_s[at, :]
        new = jnp.maximum(old, jnp.max(s, 1, keepdims=True) * scale)
        m_s[at, :] = new
        fade = jnp.exp2(old - new)
        l_s[at, :] = l_s[at, :] * fade
        acc[at, :] = acc[at, :] * fade
        add(at, s, v)

    def finish(r, count):
        blocks = count // rows
        total = jnp.sum(l_s[0:count, :], 1, keepdims=True)
        total = jnp.broadcast_to(total, (count, hd))
        some = total > 0.0
        safe = jnp.where(some, total, 1.0)
        o = (acc[0:count, :] / safe).astype(BF16)
        o_ref[pl.ds(r * splits, blocks), 0:rows, :] = o.reshape(blocks, rows, hd)
        lse = jnp.where(some, m_s[0:count, :] + jnp.log2(safe), NEG)
        lse = lse.reshape(blocks, tl, group, hd)
        lane = lax.broadcasted_iota(jnp.int32, (1, 1, hd), 2)
        span = hd // tl
        both = lse[:, tl - 1]
        for i in range(tl - 2, -1, -1):
            both = jnp.where(lane < (i + 1) * span, lse[:, i], both)
        high = both.astype(BF16).astype(F32)
        mid = (both - high).astype(BF16).astype(F32)
        low = both - high - mid
        inner = lane % span
        stat = jnp.where(inner == 0, high, jnp.where(inner == 1, mid, low))
        o_ref[pl.ds(r * splits, blocks), rows : rows + group, :] = stat.astype(BF16)
        return total

    def own_scores(r, count):
        for b in range(count // rows):
            for i in range(tl):
                q = x_ref[r * splits + b, i * group : (i + 1) * group, :].astype(F32)
                key = x_ref[r * splits + b, rows + i : rows + i + 1, :].astype(F32)
                s = jnp.sum(q * key, 1, keepdims=True) * scale
                at = b * rows + i * group
                m_s[at : at + group, :] = jnp.broadcast_to(s, (group, hd))

    def request(r, count):
        n = cnt[r]
        at = slice(0, count)
        l_s[...] = jnp.zeros_like(l_s)
        acc[...] = jnp.zeros_like(acc)

        @pl.when(r == tree_request)
        def _():
            own_scores(r, full_rows)
            first, s, v = tree_page()
            add(pl.ds(first, tree_rows), s, v)

        @pl.when(r != tree_request)
        def _():
            own_scores(r, count)

        q = queries(r, count)

        def take(start, nb):
            k, v, bias = block_of(r, n, start, nb)
            s = lax.dot_general(q, k, NT, preferred_element_type=F32)
            add(at, s + bias, v)

        eights = n // 8

        @pl.loop(0, eights)
        def _(b):
            take(b * 8, 8)

        left = (n - eights * 8 + 1) // 2
        start = eights * 8
        for size, when in (
            (8, left == 4),
            (4, (left == 2) | (left == 3)),
        ):

            @pl.when(when)
            def _():
                take(start, size)

        @pl.when((left == 1) | (left == 3))
        def _():
            take(start + jnp.where(left == 3, 4, 0), 2)

        total = finish(r, count)
        high = functools.reduce(
            jnp.maximum, [total[j : j + 8] for j in range(0, count, 8)]
        )
        top[...] = jnp.maximum(top[...], high)

    def request_online(r):
        n = cnt[r]
        at = slice(0, full_rows)
        m_s[...] = jnp.full_like(m_s, NEG)
        l_s[...] = jnp.zeros_like(l_s)
        acc[...] = jnp.zeros_like(acc)

        @pl.when(r == tree_request)
        def _():
            first, s, v = tree_page()
            add_online(pl.ds(first, tree_rows), s, v)

        q = queries(r, full_rows)

        @pl.loop(0, (n + 1) // 2)
        def _(b):
            k, v, bias = block_of(r, n, b * 2, 2)
            s = lax.dot_general(q, k, NT, preferred_element_type=F32)
            add_online(at, s + bias, v)

        finish(r, full_rows)

    @pl.loop(0, requests)
    def _(r):
        chunks = (meta[i_tl + r] * group + CHUNK - 1) // CHUNK
        for c in range(1, full_rows // CHUNK + 1):

            @pl.when(chunks == c)
            def _():
                request(r, c * CHUNK)

    @pl.when(jnp.logical_not(jnp.max(top[...]) < HUGE))
    def _():
        @pl.loop(0, requests)
        def _(r):
            request_online(r)


def attend(meta, x, mask, key_cache, value_cache, dims):
    requests, splits, tl, group, pages, page, hd = dims
    full_rows = splits * tl * group
    smem = pl.BlockSpec(memory_space=pltpu.SMEM)
    vmem = pl.BlockSpec(memory_space=pltpu.VMEM)
    return pl.pallas_call(
        functools.partial(attn_kernel, dims),
        out_shape=jax.ShapeDtypeStruct(x.shape, BF16),
        in_specs=[smem, vmem, vmem, vmem, vmem],
        out_specs=vmem,
        scratch_shapes=[
            pltpu.VMEM((full_rows, hd), F32),
            pltpu.VMEM((full_rows, hd), F32),
            pltpu.VMEM((full_rows, hd), F32),
            pltpu.VMEM((8, hd), F32),
            pltpu.SMEM((requests * SLOTS,), jnp.int32),
            pltpu.SMEM((requests * SLOTS,), jnp.int32),
            pltpu.SMEM((requests,), jnp.int32),
        ],
        compiler_params=pltpu.CompilerParams(vmem_limit_bytes=40 * 2**20),
        name="attend",
    )(meta, x, mask, key_cache, value_cache)


def join_kernel(dims, where_ref, y_ref, o_ref):
    heads, splits, tl, group, hd = dims
    rows = tl * group
    span = hd // tl
    src = lax.broadcasted_iota(jnp.int32, (hd, tl * hd), 0)
    dst = lax.broadcasted_iota(jnp.int32, (hd, tl * hd), 1)
    pick = (src // span == dst // hd) & (src % span < 3)
    pick = pick.astype(F32).astype(BF16)
    first = where_ref[0]
    length = where_ref[1]
    for h in range(heads):
        stat = y_ref[h * splits : (h + 1) * splits, rows : rows + group, :]
        lse = jnp.dot(
            stat.reshape(splits * group, hd), pick, preferred_element_type=F32
        )
        for i in range(tl):
            one = lse[:, i * hd : (i + 1) * hd].reshape(splits, group, hd)
            high = jnp.max(one, 0, keepdims=True)
            w = jnp.exp2(one - high)
            o = y_ref[
                h * splits : (h + 1) * splits, i * group : (i + 1) * group, :
            ].astype(F32)
            res = jnp.sum(w * o, 0) / jnp.sum(w, 0)
            res = jnp.where(first + i < length, res, 0.0)
            o_ref[0, i, h * group : (h + 1) * group, :] = res.astype(BF16)


def join(where, y, dims):
    heads, splits, tl, group, hd = dims
    return pl.pallas_call(
        functools.partial(join_kernel, dims),
        out_shape=jax.ShapeDtypeStruct((1, tl, heads * group, hd), BF16),
        in_specs=[
            pl.BlockSpec(memory_space=pltpu.SMEM),
            pl.BlockSpec(memory_space=pltpu.VMEM),
        ],
        out_specs=pl.BlockSpec(memory_space=pltpu.VMEM),
        name="join",
    )(where, y)


def per_device(
    queries,
    tree_keys,
    tree_values,
    key_cache,
    value_cache,
    page_request,
    page_index,
    ctx_len,
    tree_len,
    tree_mask,
):
    heads = lax.axis_size("kvh")
    splits = lax.axis_size("split")
    unused, tl, hq, hd = queries.shape
    group = hq // heads
    requests = ctx_len.shape[0]
    unused, pages, page, unused = key_cache.shape
    me = lax.axis_index("split").astype(jnp.int32)

    q = queries.reshape(tl, heads, group, hd).transpose(1, 0, 2, 3)
    x = jnp.concatenate(
        [
            q.reshape(heads, tl * group, hd),
            tree_keys[0].transpose(1, 0, 2),
            tree_values[0].transpose(1, 0, 2),
        ],
        1,
    )
    block = x.shape[1]
    x = jnp.broadcast_to(x[:, None], (heads, splits, block, hd))
    x = x.reshape(heads * splits, block, hd)
    x = lax.all_to_all(x, BOTH, 0, 0, tiled=True)

    meta = jnp.concatenate([page_request, page_index, ctx_len, tree_len, me[None]])
    dims = (requests, splits, tl, group, pages, page, hd)
    y = attend(meta, x, tree_mask, key_cache, value_cache, dims)

    y = lax.all_to_all(y, BOTH, 0, 0, tiled=True)
    own = lax.axis_index("kvh")
    where = jnp.stack([me * tl, jnp.take(tree_len, own)])
    return join(where, y, (heads, splits, tl, group, hd))


def solution(mesh):
    shard = P("kvh", "split", None, None)
    return jax.shard_map(
        per_device,
        mesh=mesh,
        in_specs=(shard,) * 5 + (P("split"), P("split"), P(), P(), P()),
        out_specs=shard,
        check_vma=False,
    )
```

time: 733 us -> 140 us (0.19)
  matrix products: 262 us -> 0 us
  waiting for transfers between devices: 151 us -> 41 us
  local copies, waits for them, and re-layouts: 113 us -> 7.42 us
  blocking collectives: 99.6 us -> 0 us
  other arithmetic: 75.8 us -> 0.63 us
  Pallas kernels: 0 us -> 72.9 us
  between operations: 13.5 us -> 0.73 us
    dot_general x98 -> x0, matrix products: 262 us -> none  [the longest x24 146 us: cache_block(): jnp.einsum('ht,hcg->tcg', one_hot_select, partial_output, precision=lax.P...]
    all_gather x2 -> x0, waiting for transfers between devices: 143 us -> none  [the longest x1 102 us: joined(): everything = jax.tree.map(lambda part: lax.all_gather(part, axis), value)]
    gather x72 -> x0, local copies, waits for them, and re-layouts: 92 us -> none  [the longest x24 47.4 us: cache_block(): selected_rows = jnp.take(q_rows, owner, axis=0)]
    all_gather x4 -> x0, blocking collectives: 79.5 us -> none  [the longest x2 42.7 us: joined(): everything = jax.tree.map(lambda part: lax.all_gather(part, axis), value)]
    pallas_call x0 -> x2, Pallas kernels: none -> 72.9 us  [the longest x1 70.2 us: attend(): pl.pallas_call(functools.partial(attn_kernel, dims), out_shape=jax.ShapeD...]
    add x32 -> x0, other arithmetic: 52.2 us -> none  [the longest x15 40.1 us: join_partials(): acc_one * f_one[..., None] + acc_two * f_two[..., None]]
    all_to_all x2, waiting for transfers between devices: 7.87 us -> 41 us  [the longest x1 21.4 us: per_device(): x = lax.all_to_all(x, BOTH, 0, 0, tiled=True)]
    all_to_all x2 -> x0, blocking collectives: 20.2 us -> none  [the longest x1 10.6 us: per_device(): lax.all_to_all(queries, 'kvh', split_axis=2, concat_axis=0, tiled=True)]
  transfers between devices with their start and end apart: 4 -> 2, of which waited for: 4 -> 2; matrix products, arithmetic and copies ran while one was open for 1% -> 1% of each run, Pallas kernels for 0% -> 0%
where the time goes in v1:
time: 140 us; the launch traced here: 139 us
  Pallas kernels  72.9 us (52%)
  waiting for transfers between devices  41 us (29%)
  starting transfers between devices  16.7 us (12%)
  local copies, waits for them, and re-layouts  7.42 us (5%)
    pallas_call x1, Pallas kernels, attend(): pl.pallas_call(functools.partial(attn_kernel, dims), out_shape=jax.ShapeD...  70.2 us
    all_to_all x1, waiting for transfers between devices, per_device(): x = lax.all_to_all(x, BOTH, 0, 0, tiled=True)  21.4 us
    all_to_all x1, waiting for transfers between devices, per_device(): y = lax.all_to_all(y, BOTH, 0, 0, tiled=True)  19.6 us
    all_to_all x1, starting transfers between devices, per_device(): x = lax.all_to_all(x, BOTH, 0, 0, tiled=True)  11.5 us
    all_to_all x1, starting transfers between devices, per_device(): y = lax.all_to_all(y, BOTH, 0, 0, tiled=True)  5.15 us
    unnamed x16, local copies, waits for them, and re-layouts  4.73 us
  transfers between devices with their start and end apart: 2, of which 2 were waited for; matrix products, arithmetic and copies ran while one was open for 1% of the time, Pallas kernels for 0%

profile of v1, /device:TPU:1, one launch (start us, length us, event | category | flops | bytes accessed | tf_op | source)
XLA Modules:
  0.0 139.4 jit_solution(2640337358223616376)
XLA Ops:
  0.0 0.0 copy-start
  0.0 0.8 copy-done
  0.9 0.7 copy_bitcast_fusion.1
  1.6 1.3 broadcast_in_dim.15
  2.9 0.0 copy-start.4
  2.9 0.0 copy-start.5
  2.9 0.0 copy-start.6
  2.9 0.0 copy-start.7
  2.9 0.0 copy-start.2
  2.9 11.5 %all-to-all-start = ((bf16[128,40,128]{2,1,0:T(8,128)(2,1)}), bf16[128,40,128]{2,1,0:T(8,128)(2,1)S(1)}, u32[]{:S(2)}, u32[]{:S(2)}) async-start(bf16[128,40,128]{2,1,0:T(8,128)(2,1)} %bitcast.10), calls=%async_computation | async-start | bytes 2621440 | tf_op jit(solution)/shard_map/all_to_all | solution.py:344
  14.4 0.0 copy-done.4
  14.4 0.0 copy-done.5
  14.4 0.0 copy-done.6
  14.4 0.0 copy-done.7
  14.4 0.1 concatenate.6.meta
  14.5 21.4 %all-to-all-done.x_ref = bf16[128,40,128]{2,1,0:T(8,128)(2,1)S(1)} async-done(((bf16[128,40,128]{2,1,0:T(8,128)(2,1)}), bf16[128,40,128]{2,1,0:T(8,128)(2,1)S(1)}, u32[]{:S(2)}, u32[]{:S(2)}) %all-to-all-start) | async-done | bytes 1310752 | tf_op jit(solution)/shard_map/all_to_all | solution.py:344
  35.9 0.0 copy-done.2
  35.9 0.0 copy-start.1
  35.9 2.8 %copy-done.1 = bf16[1,192,128,128]{3,2,1,0:T(8,128)(2,1)S(1)} copy-done((bf16[1,192,128,128]{3,2,1,0:T(8,128)(2,1)S(1)}, bf16[1,192,128,128]{3,2,1,0:T(8,128)(2,1)}, u32[]{:S(2)}) %copy-start.1) | copy-done | bytes 6291480
  38.7 70.2 %attend.1 = bf16[128,40,128]{2,1,0:T(8,128)(2,1)} custom-call(s32[401]{0:T(512)S(1)} %concatenate.6.meta, bf16[128,40,128]{2,1,0:T(8,128)(2,1)S(1)} %all-to-all-done.x_ref, s32[8,64,64]{2,1,0:T(8,128)S(1)} %copy-done.2, bf16[1,192,128,128]{3,2,1,0:T(8,128)(2,1)S(1)} %copy-done.1, bf16[1,192,128,128]{3,2,1,0:T(8,128)(2,1)} %v_ref.1), custom_call_target="tpu_custom_call" | custom-call | tf_op jit(solution)/shard_map/attend/pallas_call | solution.py:252
  108.9 5.2 %all-to-all-start.1 = ((bf16[128,40,128]{2,1,0:T(8,128)(2,1)}), bf16[128,40,128]{2,1,0:T(8,128)(2,1)S(1)}, u32[]{:S(2)}, u32[]{:S(2)}) async-start(bf16[128,40,128]{2,1,0:T(8,128)(2,1)} %attend.1), calls=%async_computation.1 | async-start | bytes 2621440 | tf_op jit(solution)/shard_map/all_to_all | solution.py:350
  114.1 0.6 dynamic-slice.2
  115.3 0.6 pad_add_fusion.where_ref
  115.9 19.6 %all-to-all-done.1.y_ref = bf16[128,40,128]{2,1,0:T(8,128)(2,1)S(1)} async-done(((bf16[128,40,128]{2,1,0:T(8,128)(2,1)}), bf16[128,40,128]{2,1,0:T(8,128)(2,1)S(1)}, u32[]{:S(2)}, u32[]{:S(2)}) %all-to-all-start.1) | async-done | bytes 1310752 | tf_op jit(solution)/shard_map/all_to_all | solution.py:350
  135.6 0.0 copy-start.3
  135.6 1.1 copy-done.3
  136.7 2.7 %join.1 = bf16[1,4,64,128]{3,2,1,0:T(8,128)(2,1)} custom-call(s32[2]{0:T(128)} %pad_add_fusion.where_ref, bf16[128,40,128]{2,1,0:T(8,128)(2,1)} %copy-done.3), custom_call_target="tpu_custom_call" | custom-call | tf_op jit(solution)/shard_map/join/pallas_call | solution.py:300
  (2 shorter events, 0.0 us)
Async XLA Ops:
  0.0 0.8 copy-start
  2.9 11.5 %copy-start.4 = (s32[192]{0:T(256)S(1)}, s32[192]{0:T(256)}, u32[]{:S(2)}) copy-start(s32[192]{0:T(256)} %param.15) | copy-start | bytes 2308
  2.9 11.5 %copy-start.5 = (s32[192]{0:T(256)S(1)}, s32[192]{0:T(256)}, u32[]{:S(2)}) copy-start(s32[192]{0:T(256)} %param.16) | copy-start | bytes 2308
  2.9 11.6 %copy-start.6 = (s32[8]{0:T(128)S(1)}, s32[8]{0:T(128)}, u32[]{:S(2)}) copy-start(s32[8]{0:T(128)} %param.17) | copy-start | bytes 100
  2.9 11.6 %copy-start.7 = (s32[8]{0:T(128)S(1)}, s32[8]{0:T(128)}, u32[]{:S(2)}) copy-start(s32[8]{0:T(128)} %param.18) | copy-start | bytes 100
  2.9 33.0 %copy-start.2 = (s32[8,64,64]{2,1,0:T(8,128)S(1)}, s32[8,64,64]{2,1,0:T(8,128)}, u32[]{:S(2)}) copy-start(s32[8,64,64]{2,1,0:T(8,128)} %mask_ref.1) | copy-start | bytes 393220
  2.9 33.0 %all-to-all-start = ((bf16[128,40,128]{2,1,0:T(8,128)(2,1)}), bf16[128,40,128]{2,1,0:T(8,128)(2,1)S(1)}, u32[]{:S(2)}, u32[]{:S(2)}) async-start(bf16[128,40,128]{2,1,0:T(8,128)(2,1)} %bitcast.10), calls=%async_computation | async-start | bytes 2621440 | tf_op jit(solution)/shard_map/all_to_all | solution.py:344
  35.9 2.8 %copy-start.1 = (bf16[1,192,128,128]{3,2,1,0:T(8,128)(2,1)S(1)}, bf16[1,192,128,128]{3,2,1,0:T(8,128)(2,1)}, u32[]{:S(2)}) copy-start(bf16[1,192,128,128]{3,2,1,0:T(8,128)(2,1)} %k_ref.1) | copy-start | bytes 18874372
  108.9 26.7 %all-to-all-start.1 = ((bf16[128,40,128]{2,1,0:T(8,128)(2,1)}), bf16[128,40,128]{2,1,0:T(8,128)(2,1)S(1)}, u32[]{:S(2)}, u32[]{:S(2)}) async-start(bf16[128,40,128]{2,1,0:T(8,128)(2,1)} %attend.1), calls=%async_computation.1 | async-start | bytes 2621440 | tf_op jit(solution)/shard_map/all_to_all | solution.py:350
  135.6 1.1 copy-start.3

commit v2 on v1

--- a/solution.py
+++ b/solution.py
@@ -11,8 +11,8 @@
 NEG = -1e30
 LOG2E = 1.4426950408889634
 HUGE = 2.0**100
-CHUNK = 128
-SLOTS = 256
+STEP = 16
+CHUNK = 64
 F32 = jnp.float32
 BF16 = jnp.bfloat16
 
@@ -24,43 +24,113 @@
     return jnp.concatenate([jnp.where(col < x, 0.0, NEG) for x in lims], 1)
 
 
+def prepare_kernel(dims, meta, lists):
+    requests, splits, tl, group, pages, page, hd = dims
+    i_ctx, i_tl = 2 * pages, 2 * pages + requests
+    i_off, i_full, i_edge = pages, pages + requests + 1, pages + 2 * requests + 1
+    i_len = pages + 3 * requests + 1
+    for r in range(requests):
+        lists[i_off + r] = 0
+        lists[i_full + r] = 0
+        lists[i_edge + r] = 0
+        lists[i_len + r] = meta[i_tl + r]
+    lists[i_len + requests] = meta[i_tl + requests]
+
+    def tokens(p):
+        r = meta[p]
+        return r, meta[i_ctx + r] - meta[pages + p] * page
+
+    def count(p, carry):
+        r, lim = tokens(p)
+        lists[p] = 0
+        lists[i_full + r] += jnp.where(lim >= page, 1, 0)
+        lists[i_edge + r] += jnp.where((lim > 0) & (lim < page), lim, 0)
+        return carry
+
+    lax.fori_loop(0, pages, count, 0)
+    total = 0
+    for r in range(requests):
+        lists[i_off + r] = total
+        total += lists[i_full + r] + jnp.where(lists[i_edge + r] > 0, 1, 0)
+        lists[i_full + r] = 0
+    lists[i_off + requests] = total
+
+    def place(p, carry):
+        r, lim = tokens(p)
+        n = lists[i_full + r]
+        whole = lim >= page
+
+        @pl.when(whole)
+        def _():
+            lists[lists[i_off + r] + n] = p
+            lists[i_full + r] = n + 1
+
+        @pl.when((lim > 0) & (lim < page))
+        def _():
+            lists[lists[i_off + r + 1] - 1] = p
+
+        return carry
+
+    lax.fori_loop(0, pages, place, 0)
+
+
+def prepare(meta, dims):
+    requests, splits, tl, group, pages, page, hd = dims
+    smem = pl.BlockSpec(memory_space=pltpu.SMEM)
+    return pl.pallas_call(
+        functools.partial(prepare_kernel, dims),
+        out_shape=jax.ShapeDtypeStruct((pages + 4 * requests + 2,), jnp.int32),
+        in_specs=[smem],
+        out_specs=smem,
+        compiler_params=pltpu.CompilerParams(vmem_limit_bytes=2**20),
+        cost_estimate=pl.CostEstimate(
+            flops=0, bytes_accessed=2**24, transcendentals=0
+        ),
+        name="prepare",
+    )(meta)
+
+
 def attn_kernel(
     dims,
-    meta,
+    lists,
     x_ref,
     mask_ref,
+    k_hbm,
+    v_hbm,
+    o_ref,
     k_ref,
     v_ref,
-    o_ref,
     m_s,
     l_s,
     acc,
     top,
-    plist,
-    plim,
-    cnt,
+    sems,
 ):
     requests, splits, tl, group, pages, page, hd = dims
     rows = tl * group
     full_rows = splits * rows
     scale = hd**-0.5 * LOG2E
-    i_ctx, i_tl, i_me = 2 * pages, 2 * pages + requests, 2 * pages + 2 * requests
+    i_off, i_full, i_edge = pages, pages + requests + 1, pages + 2 * requests + 1
+    i_tl = pages + 3 * requests + 1
 
     for r in range(requests):
-        cnt[r] = 0
-
-    def scan(p, carry):
-        r = meta[p]
-        lim = meta[i_ctx + r] - meta[pages + p] * page
-        c = cnt[r]
-        plist[r * SLOTS + c] = p
-        plim[r * SLOTS + c] = lim
-        cnt[r] = jnp.where(lim > 0, c + 1, c)
-        return carry
-
-    lax.fori_loop(0, pages, scan, 0)
-
-    me = meta[i_me]
+
+        @pl.loop(lists[i_off + r], lists[i_off + r + 1])
+        def _(slot):
+            p = lists[slot]
+            pltpu.make_async_copy(k_hbm.at[0, p], k_ref.at[slot], sems.at[0, r]).start()
+            pltpu.make_async_copy(v_hbm.at[0, p], v_ref.at[slot], sems.at[1, r]).start()
+
+    def arrive(r):
+        n = lists[i_off + r + 1] - lists[i_off + r]
+
+        @pl.when(n > 0)
+        def _():
+            at = pl.ds(0, n)
+            for t, (src, dst) in enumerate(((k_hbm, k_ref), (v_hbm, v_ref))):
+                pltpu.make_async_copy(src.at[0, at], dst.at[at], sems.at[t, r]).wait()
+
+    me = lists[i_tl + requests]
     per = splits // requests
     tree_request = me // per
     part = me % per
@@ -95,19 +165,27 @@
         s = lax.dot_general(q.reshape(tree_rows, hd), kv, NT, preferred_element_type=F32)
         return first, s + bias.reshape(tree_rows, wide), values
 
-    def block_of(r, n, start, nb):
-        ids, lims = [], []
-        for j in range(nb):
-            there = start + j < n
-            at = r * SLOTS + jnp.minimum(start + j, n)
-            ids.append(jnp.where(there, plist[at], 0))
-            lims.append(jnp.where(there, plim[at], 0))
-        k = jnp.concatenate([k_ref[0, i] for i in ids], 0)
-        v = jnp.concatenate([v_ref[0, i] for i in ids], 0)
-        return k, v, column_bias(lims, page)
-
-    def add(at, s, v):
-        m = m_s[at, :]
+    def whole_block(r, start, nb):
+        at = pl.ds(lists[i_off + r] + start, nb)
+        return k_ref[at].reshape(nb * page, hd), v_ref[at].reshape(nb * page, hd)
+
+    def last_block(r):
+        n = lists[i_full + r]
+        left = n % 2
+        first = lists[i_off + r]
+        edge = lists[i_edge + r]
+        one = first + jnp.where(left == 1, n - 1, 0)
+        two = first + jnp.where(edge > 0, n, 0)
+        bias = column_bias([left * page, edge], page)
+        k = jnp.concatenate([k_ref[one], k_ref[two]], 0)
+        v = jnp.concatenate([v_ref[one], v_ref[two]], 0)
+        return k, v, bias
+
+    def has_last(r):
+        return (lists[i_full + r] % 2 == 1) | (lists[i_edge + r] > 0)
+
+    def add(at, where, s, v):
+        m = m_s[where, :]
         ps = [
             jnp.exp2(s[:, j : j + page] * scale - m) for j in range(0, s.shape[1], page)
         ]
@@ -115,14 +193,14 @@
         p = jnp.concatenate([x.astype(BF16) for x in ps], 1)
         acc[at, :] += jnp.dot(p, v, preferred_element_type=F32)
 
-    def add_online(at, s, v):
-        old = m_s[at, :]
+    def add_online(at, where, s, v):
+        old = m_s[where, :]
         new = jnp.maximum(old, jnp.max(s, 1, keepdims=True) * scale)
-        m_s[at, :] = new
+        m_s[where, :] = new
         fade = jnp.exp2(old - new)
         l_s[at, :] = l_s[at, :] * fade
         acc[at, :] = acc[at, :] * fade
-        add(at, s, v)
+        add(at, where, s, v)
 
     def finish(r, count):
         blocks = count // rows
@@ -132,7 +210,8 @@
         safe = jnp.where(some, total, 1.0)
         o = (acc[0:count, :] / safe).astype(BF16)
         o_ref[pl.ds(r * splits, blocks), 0:rows, :] = o.reshape(blocks, rows, hd)
-        lse = jnp.where(some, m_s[0:count, :] + jnp.log2(safe), NEG)
+        shift = m_s[pl.ds(r * full_rows, count), :]
+        lse = jnp.where(some, shift + jnp.log2(safe), NEG)
         lse = lse.reshape(blocks, tl, group, hd)
         lane = lax.broadcasted_iota(jnp.int32, (1, 1, hd), 2)
         span = hd // tl
@@ -147,58 +226,61 @@
         o_ref[pl.ds(r * splits, blocks), rows : rows + group, :] = stat.astype(BF16)
         return total
 
-    def own_scores(r, count):
-        for b in range(count // rows):
+    @pl.loop(0, requests)
+    def _(r):
+        for b in range(splits):
             for i in range(tl):
-                q = x_ref[r * splits + b, i * group : (i + 1) * group, :].astype(F32)
-                key = x_ref[r * splits + b, rows + i : rows + i + 1, :].astype(F32)
+                block = r * splits + b
+                q = x_ref[block, i * group : (i + 1) * group, :].astype(F32)
+                key = x_ref[block, rows + i : rows + i + 1, :].astype(F32)
                 s = jnp.sum(q * key, 1, keepdims=True) * scale
-                at = b * rows + i * group
-                m_s[at : at + group, :] = jnp.broadcast_to(s, (group, hd))
+                at = pl.multiple_of(block * rows + i * group, group)
+                m_s[pl.ds(at, group), :] = jnp.broadcast_to(s, (group, hd))
+
+    def rows_of(r, first, count):
+        return pl.ds(pl.multiple_of(r * full_rows + first, 8), count)
 
     def request(r, count):
-        n = cnt[r]
         at = slice(0, count)
+        where = rows_of(r, 0, count)
         l_s[...] = jnp.zeros_like(l_s)
         acc[...] = jnp.zeros_like(acc)
 
         @pl.when(r == tree_request)
         def _():
-            own_scores(r, full_rows)
             first, s, v = tree_page()
-            add(pl.ds(first, tree_rows), s, v)
-
-        @pl.when(r != tree_request)
-        def _():
-            own_scores(r, count)
+            add(pl.ds(first, tree_rows), rows_of(r, first, tree_rows), s, v)
 
         q = queries(r, count)
 
         def take(start, nb):
-            k, v, bias = block_of(r, n, start, nb)
+            k, v = whole_block(r, start, nb)
+            add(at, where, lax.dot_general(q, k, NT, preferred_element_type=F32), v)
+
+        n = lists[i_full + r]
+        whole = n // STEP
+
+        @pl.loop(0, whole)
+        def _(b):
+            take(b * STEP, STEP)
+
+        start = whole * STEP
+        size = STEP // 2
+        while size > 1:
+            there = (n // size) % 2
+
+            @pl.when(there == 1)
+            def _(start=start, size=size):
+                take(start, size)
+
+            start = start + there * size
+            size //= 2
+
+        @pl.when(has_last(r))
+        def _():
+            k, v, bias = last_block(r)
             s = lax.dot_general(q, k, NT, preferred_element_type=F32)
-            add(at, s + bias, v)
-
-        eights = n // 8
-
-        @pl.loop(0, eights)
-        def _(b):
-            take(b * 8, 8)
-
-        left = (n - eights * 8 + 1) // 2
-        start = eights * 8
-        for size, when in (
-            (8, left == 4),
-            (4, (left == 2) | (left == 3)),
-        ):
-
-            @pl.when(when)
-            def _():
-                take(start, size)
-
-        @pl.when((left == 1) | (left == 3))
-        def _():
-            take(start + jnp.where(left == 3, 4, 0), 2)
+            add(at, where, s + bias, v)
 
         total = finish(r, count)
         high = functools.reduce(
@@ -207,33 +289,40 @@
         top[...] = jnp.maximum(top[...], high)
 
     def request_online(r):
-        n = cnt[r]
         at = slice(0, full_rows)
-        m_s[...] = jnp.full_like(m_s, NEG)
+        where = rows_of(r, 0, full_rows)
+        m_s[where, :] = jnp.full((full_rows, hd), NEG, F32)
         l_s[...] = jnp.zeros_like(l_s)
         acc[...] = jnp.zeros_like(acc)
 
         @pl.when(r == tree_request)
         def _():
             first, s, v = tree_page()
-            add_online(pl.ds(first, tree_rows), s, v)
+            add_online(pl.ds(first, tree_rows), rows_of(r, first, tree_rows), s, v)
 
         q = queries(r, full_rows)
 
-        @pl.loop(0, (n + 1) // 2)
+        @pl.loop(0, lists[i_full + r] // 2)
         def _(b):
-            k, v, bias = block_of(r, n, b * 2, 2)
+            k, v = whole_block(r, b * 2, 2)
             s = lax.dot_general(q, k, NT, preferred_element_type=F32)
-            add_online(at, s + bias, v)
+            add_online(at, where, s, v)
+
+        @pl.when(has_last(r))
+        def _():
+            k, v, bias = last_block(r)
+            s = lax.dot_general(q, k, NT, preferred_element_type=F32)
+            add_online(at, where, s + bias, v)
 
         finish(r, full_rows)
 
     @pl.loop(0, requests)
     def _(r):
-        chunks = (meta[i_tl + r] * group + CHUNK - 1) // CHUNK
-        for c in range(1, full_rows // CHUNK + 1):
-
-            @pl.when(chunks == c)
+        arrive(r)
+        chunks = (lists[i_tl + r] * group + CHUNK - 1) // CHUNK
+        for c in range(2, full_rows // CHUNK + 1):
+
+            @pl.when((chunks == c) | ((c == 2) & (chunks < 2)))
             def _():
                 request(r, c * CHUNK)
 
@@ -244,28 +333,29 @@
             request_online(r)
 
 
-def attend(meta, x, mask, key_cache, value_cache, dims):
+def attend(lists, x, mask, key_cache, value_cache, dims):
     requests, splits, tl, group, pages, page, hd = dims
     full_rows = splits * tl * group
     smem = pl.BlockSpec(memory_space=pltpu.SMEM)
     vmem = pl.BlockSpec(memory_space=pltpu.VMEM)
+    hbm = pl.BlockSpec(memory_space=pltpu.HBM)
     return pl.pallas_call(
         functools.partial(attn_kernel, dims),
         out_shape=jax.ShapeDtypeStruct(x.shape, BF16),
-        in_specs=[smem, vmem, vmem, vmem, vmem],
+        in_specs=[smem, vmem, vmem, hbm, hbm],
         out_specs=vmem,
         scratch_shapes=[
-            pltpu.VMEM((full_rows, hd), F32),
+            pltpu.VMEM((pages, page, hd), BF16),
+            pltpu.VMEM((pages, page, hd), BF16),
+            pltpu.VMEM((requests * full_rows, hd), F32),
             pltpu.VMEM((full_rows, hd), F32),
             pltpu.VMEM((full_rows, hd), F32),
             pltpu.VMEM((8, hd), F32),
-            pltpu.SMEM((requests * SLOTS,), jnp.int32),
-            pltpu.SMEM((requests * SLOTS,), jnp.int32),
-            pltpu.SMEM((requests,), jnp.int32),
+            pltpu.SemaphoreType.DMA((2, requests)),
         ],
-        compiler_params=pltpu.CompilerParams(vmem_limit_bytes=40 * 2**20),
+        compiler_params=pltpu.CompilerParams(vmem_limit_bytes=48 * 2**20),
         name="attend",
-    )(meta, x, mask, key_cache, value_cache)
+    )(lists, x, mask, key_cache, value_cache)
 
 
 def join_kernel(dims, where_ref, y_ref, o_ref):
@@ -305,6 +395,7 @@
             pl.BlockSpec(memory_space=pltpu.VMEM),
         ],
         out_specs=pl.BlockSpec(memory_space=pltpu.VMEM),
+        compiler_params=pltpu.CompilerParams(vmem_limit_bytes=16 * 2**20),
         name="join",
     )(where, y)
 
@@ -345,7 +436,8 @@
 
     meta = jnp.concatenate([page_request, page_index, ctx_len, tree_len, me[None]])
     dims = (requests, splits, tl, group, pages, page, hd)
-    y = attend(meta, x, tree_mask, key_cache, value_cache, dims)
+    lists = prepare(meta, dims)
+    y = attend(lists, x, tree_mask, key_cache, value_cache, dims)
 
     y = lax.all_to_all(y, BOTH, 0, 0, tiled=True)
     own = lax.axis_index("kvh")

time: 140 us -> 130 us (0.929)
  waiting for transfers between devices: 41 us -> 32.8 us
  local copies, waits for them, and re-layouts: 7.42 us -> 3.59 us
  Pallas kernels: 72.9 us -> 76.4 us
    all_to_all x1, waiting for transfers between devices: 21.4 us -> 12.6 us  [per_device(): x = lax.all_to_all(x, BOTH, 0, 0, tiled=True)]
    pallas_call x0 -> x1, Pallas kernels: none -> 8.78 us  [prepare(): pl.pallas_call(functools.partial(prepare_kernel, dims), out_shape=jax.Sha...]
    pallas_call x1, Pallas kernels: 70.2 us -> 65.7 us  [attend(): pl.pallas_call(functools.partial(attn_kernel, dims), out_shape=jax.ShapeD...]
    unnamed x16 -> x12, local copies, waits for them, and re-layouts: 4.73 us -> 0.86 us
  transfers between devices with their start and end apart: 2 -> 2, of which waited for: 2 -> 2; matrix products, arithmetic and copies ran while one was open for 1% -> 1% of each run, Pallas kernels for 0% -> 7%
where the time goes in v2:
time: 130 us
  Pallas kernels  76.4 us (59%)
  waiting for transfers between devices  32.8 us (25%)
  starting transfers between devices  16.8 us (13%)
  local copies, waits for them, and re-layouts  3.59 us (3%)
    pallas_call x1, Pallas kernels, attend(): pl.pallas_call(functools.partial(attn_kernel, dims), out_shape=jax.ShapeD...  65.7 us
    all_to_all x1, waiting for transfers between devices, per_device(): y = lax.all_to_all(y, BOTH, 0, 0, tiled=True)  20.2 us
    all_to_all x1, waiting for transfers between devices, per_device(): x = lax.all_to_all(x, BOTH, 0, 0, tiled=True)  12.6 us
    all_to_all x1, starting transfers between devices, per_device(): x = lax.all_to_all(x, BOTH, 0, 0, tiled=True)  11.5 us
    pallas_call x1, Pallas kernels, prepare(): pl.pallas_call(functools.partial(prepare_kernel, dims), out_shape=jax.Sha...  8.78 us
    all_to_all x1, starting transfers between devices, per_device(): y = lax.all_to_all(y, BOTH, 0, 0, tiled=True)  5.32 us
  transfers between devices with their start and end apart: 2, of which 2 were waited for; matrix products, arithmetic and copies ran while one was open for 1% of the time, Pallas kernels for 7%

profile of v2, /device:TPU:1, one launch (start us, length us, event | category | flops | bytes accessed | tf_op | source)
XLA Modules:
  0.0 130.4 jit_solution(16309633193120250979)
XLA Ops:
  0.0 0.0 copy-start
  0.0 0.8 copy-done
  0.9 0.7 copy_bitcast_fusion.1
  1.6 1.3 broadcast_in_dim.15
  2.9 0.0 copy-start.2
  2.9 0.0 copy-start.3
  2.9 0.0 copy-start.4
  2.9 0.0 copy-start.5
  2.9 0.0 copy-start.1
  2.9 11.5 %all-to-all-start = ((bf16[128,40,128]{2,1,0:T(8,128)(2,1)}), bf16[128,40,128]{2,1,0:T(8,128)(2,1)S(1)}, u32[]{:S(2)}, u32[]{:S(2)}) async-start(bf16[128,40,128]{2,1,0:T(8,128)(2,1)} %bitcast.10), calls=%async_computation | async-start | bytes 2621440 | tf_op jit(solution)/shard_map/all_to_all | solution.py:435
  14.4 0.0 copy-done.2
  14.4 0.0 copy-done.3
  14.4 0.0 copy-done.4
  14.4 0.0 copy-done.5
  14.4 0.1 concatenate.6.meta
  14.5 8.8 %prepare.1.lists = s32[226]{0:T(256)S(1)} custom-call(s32[401]{0:T(512)S(1)} %concatenate.6.meta), custom_call_target="tpu_custom_call" | custom-call | bytes 16777216 | tf_op jit(solution)/shard_map/prepare/pallas_call | solution.py:80
  23.3 12.6 %all-to-all-done.x_ref = bf16[128,40,128]{2,1,0:T(8,128)(2,1)S(1)} async-done(((bf16[128,40,128]{2,1,0:T(8,128)(2,1)}), bf16[128,40,128]{2,1,0:T(8,128)(2,1)S(1)}, u32[]{:S(2)}, u32[]{:S(2)}) %all-to-all-start) | async-done | bytes 1310752 | tf_op jit(solution)/shard_map/all_to_all | solution.py:435
  35.9 0.0 copy-done.1
  35.9 65.7 %attend.1 = bf16[128,40,128]{2,1,0:T(8,128)(2,1)} custom-call(s32[226]{0:T(256)S(1)} %prepare.1.lists, bf16[128,40,128]{2,1,0:T(8,128)(2,1)S(1)} %all-to-all-done.x_ref, s32[8,64,64]{2,1,0:T(8,128)S(1)} %copy-done.1, bf16[1,192,128,128]{3,2,1,0:T(8,128)(2,1)} %k_hbm.1, bf16[1,192,128,128]{3,2,1,0:T(8,128)(2,1)} %v_hbm.1), custom_call_target="tpu_custom_call" | custom-call | tf_op jit(solution)/shard_map/attend/pallas_call | solution.py:342
  101.6 5.3 %all-to-all-start.1 = ((bf16[128,40,128]{2,1,0:T(8,128)(2,1)}), bf16[128,40,128]{2,1,0:T(8,128)(2,1)S(1)}, u32[]{:S(2)}, u32[]{:S(2)}) async-start(bf16[128,40,128]{2,1,0:T(8,128)(2,1)} %attend.1), calls=%async_computation.1 | async-start | bytes 2621440 | tf_op jit(solution)/shard_map/all_to_all | solution.py:442
  107.0 0.6 dynamic-slice.2
  108.2 0.1 pad_add_fusion.where_ref
  108.3 20.2 %all-to-all-done.1.y_ref = bf16[128,40,128]{2,1,0:T(8,128)(2,1)S(1)} async-done(((bf16[128,40,128]{2,1,0:T(8,128)(2,1)}), bf16[128,40,128]{2,1,0:T(8,128)(2,1)S(1)}, u32[]{:S(2)}, u32[]{:S(2)}) %all-to-all-start.1) | async-done | bytes 1310752 | tf_op jit(solution)/shard_map/all_to_all | solution.py:442
  128.5 1.9 %join.1 = bf16[1,4,64,128]{3,2,1,0:T(8,128)(2,1)} custom-call(s32[2]{0:T(128)S(1)} %pad_add_fusion.where_ref, bf16[128,40,128]{2,1,0:T(8,128)(2,1)S(1)} %all-to-all-done.1.y_ref), custom_call_target="tpu_custom_call" | custom-call | tf_op jit(solution)/shard_map/join/pallas_call | solution.py:390
  (2 shorter events, 0.0 us)
Async XLA Ops:
  0.0 0.8 copy-start
  2.9 11.5 %copy-start.2 = (s32[192]{0:T(256)S(1)}, s32[192]{0:T(256)}, u32[]{:S(2)}) copy-start(s32[192]{0:T(256)} %param.15) | copy-start | bytes 2308
  2.9 11.5 %copy-start.3 = (s32[192]{0:T(256)S(1)}, s32[192]{0:T(256)}, u32[]{:S(2)}) copy-start(s32[192]{0:T(256)} %param.16) | copy-start | bytes 2308
  2.9 11.6 %copy-start.4 = (s32[8]{0:T(128)S(1)}, s32[8]{0:T(128)}, u32[]{:S(2)}) copy-start(s32[8]{0:T(128)} %param.17) | copy-start | bytes 100
  2.9 11.6 %copy-start.5 = (s32[8]{0:T(128)S(1)}, s32[8]{0:T(128)}, u32[]{:S(2)}) copy-start(s32[8]{0:T(128)} %param.18) | copy-start | bytes 100
  2.9 33.0 %copy-start.1 = (s32[8,64,64]{2,1,0:T(8,128)S(1)}, s32[8,64,64]{2,1,0:T(8,128)}, u32[]{:S(2)}) copy-start(s32[8,64,64]{2,1,0:T(8,128)} %mask_ref.1) | copy-start | bytes 393220
  2.9 33.0 %all-to-all-start = ((bf16[128,40,128]{2,1,0:T(8,128)(2,1)}), bf16[128,40,128]{2,1,0:T(8,128)(2,1)S(1)}, u32[]{:S(2)}, u32[]{:S(2)}) async-start(bf16[128,40,128]{2,1,0:T(8,128)(2,1)} %bitcast.10), calls=%async_computation | async-start | bytes 2621440 | tf_op jit(solution)/shard_map/all_to_all | solution.py:435
  101.6 26.8 %all-to-all-start.1 = ((bf16[128,40,128]{2,1,0:T(8,128)(2,1)}), bf16[128,40,128]{2,1,0:T(8,128)(2,1)S(1)}, u32[]{:S(2)}, u32[]{:S(2)}) async-start(bf16[128,40,128]{2,1,0:T(8,128)(2,1)} %attend.1), calls=%async_computation.1 | async-start | bytes 2621440 | tf_op jit(solution)/shard_map/all_to_all | solution.py:442

commit v3 on v2

--- a/solution.py
+++ b/solution.py
@@ -12,6 +12,7 @@
 LOG2E = 1.4426950408889634
 HUGE = 2.0**100
 STEP = 16
+TAIL = 4
 CHUNK = 64
 F32 = jnp.float32
 BF16 = jnp.bfloat16
@@ -22,6 +23,44 @@
 def column_bias(lims, page):
     col = lax.broadcasted_iota(jnp.int32, (1, page), 1)
     return jnp.concatenate([jnp.where(col < x, 0.0, NEG) for x in lims], 1)
+
+
+def pack_kernel(dims, q_ref, tk_ref, tv_ref, o_ref, block, sems):
+    heads, splits, tl, group, hd = dims
+    tk = tk_ref[0].astype(F32)
+    tv = tv_ref[0].astype(F32)
+    for h in range(heads):
+        for i in range(tl):
+            block[h, i * group : (i + 1) * group, :] = q_ref[
+                0, i, h * group : (h + 1) * group, :
+            ]
+        both = [t[i, h : h + 1] for t in (tk, tv) for i in range(tl)]
+        block[h, tl * group :, :] = jnp.concatenate(both, 0).astype(BF16)
+    copies = [
+        pltpu.make_async_copy(block, o_ref.at[:, s], sems.at[s]) for s in range(splits)
+    ]
+    for c in copies:
+        c.start()
+    for c in copies:
+        c.wait()
+
+
+def pack(queries, tree_keys, tree_values, dims):
+    heads, splits, tl, group, hd = dims
+    rows = tl * group + 2 * tl
+    vmem = pl.BlockSpec(memory_space=pltpu.VMEM)
+    return pl.pallas_call(
+        functools.partial(pack_kernel, dims),
+        out_shape=jax.ShapeDtypeStruct((heads, splits, rows, hd), BF16),
+        in_specs=[vmem, vmem, vmem],
+        out_specs=pl.BlockSpec(memory_space=pltpu.HBM),
+        scratch_shapes=[
+            pltpu.VMEM((heads, rows, hd), BF16),
+            pltpu.SemaphoreType.DMA((splits,)),
+        ],
+        compiler_params=pltpu.CompilerParams(vmem_limit_bytes=8 * 2**20),
+        name="pack",
+    )(queries, tree_keys, tree_values)
 
 
 def prepare_kernel(dims, meta, lists):
@@ -169,20 +208,22 @@
         at = pl.ds(lists[i_off + r] + start, nb)
         return k_ref[at].reshape(nb * page, hd), v_ref[at].reshape(nb * page, hd)
 
-    def last_block(r):
-        n = lists[i_full + r]
-        left = n % 2
-        first = lists[i_off + r]
+    def pages_of(r):
+        return lists[i_off + r + 1] - lists[i_off + r]
+
+    def last_block(r, start, nb):
+        n = pages_of(r)
         edge = lists[i_edge + r]
-        one = first + jnp.where(left == 1, n - 1, 0)
-        two = first + jnp.where(edge > 0, n, 0)
-        bias = column_bias([left * page, edge], page)
-        k = jnp.concatenate([k_ref[one], k_ref[two]], 0)
-        v = jnp.concatenate([v_ref[one], v_ref[two]], 0)
-        return k, v, bias
-
-    def has_last(r):
-        return (lists[i_full + r] % 2 == 1) | (lists[i_edge + r] > 0)
+        ids, lims = [], []
+        for j in range(nb):
+            at = start + j
+            ids.append(lists[i_off + r] + jnp.minimum(at, n - 1))
+            lims.append(
+                jnp.where(at < lists[i_full + r], page, jnp.where(at < n, edge, 0))
+            )
+        k = jnp.concatenate([k_ref[i] for i in ids], 0)
+        v = jnp.concatenate([v_ref[i] for i in ids], 0)
+        return k, v, column_bias(lims, page)
 
     def add(at, where, s, v):
         m = m_s[where, :]
@@ -257,30 +298,21 @@
             k, v = whole_block(r, start, nb)
             add(at, where, lax.dot_general(q, k, NT, preferred_element_type=F32), v)
 
-        n = lists[i_full + r]
-        whole = n // STEP
+        whole = lists[i_full + r] // STEP
 
         @pl.loop(0, whole)
         def _(b):
             take(b * STEP, STEP)
 
         start = whole * STEP
-        size = STEP // 2
-        while size > 1:
-            there = (n // size) % 2
-
-            @pl.when(there == 1)
-            def _(start=start, size=size):
-                take(start, size)
-
-            start = start + there * size
-            size //= 2
-
-        @pl.when(has_last(r))
-        def _():
-            k, v, bias = last_block(r)
-            s = lax.dot_general(q, k, NT, preferred_element_type=F32)
-            add(at, where, s + bias, v)
+        quarters = (pages_of(r) - start + TAIL - 1) // TAIL
+        for c in range(1, STEP // TAIL + 1):
+
+            @pl.when(quarters == c)
+            def _(c=c):
+                k, v, bias = last_block(r, start, c * TAIL)
+                s = lax.dot_general(q, k, NT, preferred_element_type=F32)
+                add(at, where, s + bias, v)
 
         total = finish(r, count)
         high = functools.reduce(
@@ -302,15 +334,9 @@
 
         q = queries(r, full_rows)
 
-        @pl.loop(0, lists[i_full + r] // 2)
+        @pl.loop(0, (pages_of(r) + 1) // 2)
         def _(b):
-            k, v = whole_block(r, b * 2, 2)
-            s = lax.dot_general(q, k, NT, preferred_element_type=F32)
-            add_online(at, where, s, v)
-
-        @pl.when(has_last(r))
-        def _():
-            k, v, bias = last_block(r)
+            k, v, bias = last_block(r, b * 2, 2)
             s = lax.dot_general(q, k, NT, preferred_element_type=F32)
             add_online(at, where, s + bias, v)
 
@@ -420,18 +446,8 @@
     unused, pages, page, unused = key_cache.shape
     me = lax.axis_index("split").astype(jnp.int32)
 
-    q = queries.reshape(tl, heads, group, hd).transpose(1, 0, 2, 3)
-    x = jnp.concatenate(
-        [
-            q.reshape(heads, tl * group, hd),
-            tree_keys[0].transpose(1, 0, 2),
-            tree_values[0].transpose(1, 0, 2),
-        ],
-        1,
-    )
-    block = x.shape[1]
-    x = jnp.broadcast_to(x[:, None], (heads, splits, block, hd))
-    x = x.reshape(heads * splits, block, hd)
+    x = pack(queries, tree_keys, tree_values, (heads, splits, tl, group, hd))
+    x = x.reshape((heads * splits,) + x.shape[2:])
     x = lax.all_to_all(x, BOTH, 0, 0, tiled=True)
 
     meta = jnp.concatenate([page_request, page_index, ctx_len, tree_len, me[None]])

time: 130 us -> 127 us (0.977); the launches traced: 130 us -> 125 us
  Pallas kernels: 76.4 us -> 71.7 us
    pallas_call x1, Pallas kernels: 65.7 us -> 59.7 us  [attend(): pl.pallas_call(functools.partial(attn_kernel, dims), out_shape=jax.ShapeD...]
    unnamed x12 -> x16, local copies, waits for them, and re-layouts: 0.86 us -> 2.26 us
where the time goes in v3:
time: 127 us; the launch traced here: 125 us
  Pallas kernels  71.7 us (56%)
  waiting for transfers between devices  32.8 us (26%)
  starting transfers between devices  16.6 us (13%)
  local copies, waits for them, and re-layouts  2.99 us (2%)
    pallas_call x1, Pallas kernels, attend(): pl.pallas_call(functools.partial(attn_kernel, dims), out_shape=jax.ShapeD...  59.7 us
    all_to_all x1, waiting for transfers between devices, per_device(): y = lax.all_to_all(y, BOTH, 0, 0, tiled=True)  20.2 us
    all_to_all x1, waiting for transfers between devices, per_device(): x = lax.all_to_all(x, BOTH, 0, 0, tiled=True)  12.6 us
    all_to_all x1, starting transfers between devices, per_device(): x = lax.all_to_all(x, BOTH, 0, 0, tiled=True)  11.5 us
    pallas_call x1, Pallas kernels, prepare(): pl.pallas_call(functools.partial(prepare_kernel, dims), out_shape=jax.Sha...  8.78 us
    all_to_all x1, starting transfers between devices, per_device(): y = lax.all_to_all(y, BOTH, 0, 0, tiled=True)  5.09 us
  transfers between devices with their start and end apart: 2, of which 2 were waited for; matrix products, arithmetic and copies ran while one was open for 1% of the time, Pallas kernels for 7%

profile of v3, /device:TPU:1, one launch (start us, length us, event | category | flops | bytes accessed | tf_op | source)
XLA Modules:
  0.0 124.9 jit_solution(15425685890580169033)
XLA Ops:
  0.0 0.0 copy-start.1
  0.0 0.8 copy-done.1
  0.8 0.0 copy-start.2
  0.8 0.7 copy-done.2
  1.5 0.0 copy-start.3
  1.5 0.7 copy-done.3
  2.2 1.3 %pack.1 = bf16[8,16,40,128]{3,2,1,0:T(8,128)(2,1)} custom-call(bf16[1,4,64,128]{3,2,1,0:T(8,128)(2,1)S(1)} %copy-done.1, bf16[1,4,8,128]{3,2,1,0:T(8,128)(2,1)S(1)} %copy-done.2, bf16[1,4,8,128]{3,2,1,0:T(8,128)(2,1)S(1)} %copy-done.3), custom_call_target="tpu_custom_call" | custom-call | tf_op jit(solution)/shard_map/pack/pallas_call | solution.py:52
  3.5 0.0 copy-start.4
  3.5 0.0 copy-start.5
  3.5 0.0 copy-start.6
  3.5 0.0 copy-start.7
  3.5 0.0 copy-start
  3.6 11.5 %all-to-all-start = ((bf16[128,40,128]{2,1,0:T(8,128)(2,1)}), bf16[128,40,128]{2,1,0:T(8,128)(2,1)S(1)}, u32[]{:S(2)}, u32[]{:S(2)}) async-start(bf16[128,40,128]{2,1,0:T(8,128)(2,1)} %bitcast.3), calls=%async_computation | async-start | bytes 2621440 | tf_op jit(solution)/shard_map/all_to_all | solution.py:451
  15.1 0.0 copy-done.4
  15.1 0.0 copy-done.5
  15.1 0.0 copy-done.6
  15.1 0.0 copy-done.7
  15.1 0.1 concatenate.3.meta
  15.2 8.8 %prepare.1.lists = s32[226]{0:T(256)S(1)} custom-call(s32[401]{0:T(512)S(1)} %concatenate.3.meta), custom_call_target="tpu_custom_call" | custom-call | bytes 16777216 | tf_op jit(solution)/shard_map/prepare/pallas_call | solution.py:119
  24.0 12.6 %all-to-all-done.x_ref = bf16[128,40,128]{2,1,0:T(8,128)(2,1)S(1)} async-done(((bf16[128,40,128]{2,1,0:T(8,128)(2,1)}), bf16[128,40,128]{2,1,0:T(8,128)(2,1)S(1)}, u32[]{:S(2)}, u32[]{:S(2)}) %all-to-all-start) | async-done | bytes 1310752 | tf_op jit(solution)/shard_map/all_to_all | solution.py:451
  36.6 0.0 copy-done
  36.6 59.7 %attend.1 = bf16[128,40,128]{2,1,0:T(8,128)(2,1)} custom-call(s32[226]{0:T(256)S(1)} %prepare.1.lists, bf16[128,40,128]{2,1,0:T(8,128)(2,1)S(1)} %all-to-all-done.x_ref, s32[8,64,64]{2,1,0:T(8,128)S(1)} %copy-done, bf16[1,192,128,128]{3,2,1,0:T(8,128)(2,1)} %k_hbm.1, bf16[1,192,128,128]{3,2,1,0:T(8,128)(2,1)} %v_hbm.1), custom_call_target="tpu_custom_call" | custom-call | tf_op jit(solution)/shard_map/attend/pallas_call | solution.py:368
  96.3 5.1 %all-to-all-start.1 = ((bf16[128,40,128]{2,1,0:T(8,128)(2,1)}), bf16[128,40,128]{2,1,0:T(8,128)(2,1)S(1)}, u32[]{:S(2)}, u32[]{:S(2)}) async-start(bf16[128,40,128]{2,1,0:T(8,128)(2,1)} %attend.1), calls=%async_computation.1 | async-start | bytes 2621440 | tf_op jit(solution)/shard_map/all_to_all | solution.py:458
  101.4 0.6 dynamic-slice.2
  102.7 0.1 pad_add_fusion.where_ref
  102.8 20.2 %all-to-all-done.1.y_ref = bf16[128,40,128]{2,1,0:T(8,128)(2,1)S(1)} async-done(((bf16[128,40,128]{2,1,0:T(8,128)(2,1)}), bf16[128,40,128]{2,1,0:T(8,128)(2,1)S(1)}, u32[]{:S(2)}, u32[]{:S(2)}) %all-to-all-start.1) | async-done | bytes 1310752 | tf_op jit(solution)/shard_map/all_to_all | solution.py:458
  122.9 1.9 %join.1 = bf16[1,4,64,128]{3,2,1,0:T(8,128)(2,1)} custom-call(s32[2]{0:T(128)S(1)} %pad_add_fusion.where_ref, bf16[128,40,128]{2,1,0:T(8,128)(2,1)S(1)} %all-to-all-done.1.y_ref), custom_call_target="tpu_custom_call" | custom-call | tf_op jit(solution)/shard_map/join/pallas_call | solution.py:416
Async XLA Ops:
  0.0 0.8 copy-start.1
  0.8 0.7 copy-start.2
  1.5 0.7 copy-start.3
  3.5 11.6 %copy-start.4 = (s32[192]{0:T(256)S(1)}, s32[192]{0:T(256)}, u32[]{:S(2)}) copy-start(s32[192]{0:T(256)} %param.15) | copy-start | bytes 2308
  3.5 11.6 %copy-start.5 = (s32[192]{0:T(256)S(1)}, s32[192]{0:T(256)}, u32[]{:S(2)}) copy-start(s32[192]{0:T(256)} %param.16) | copy-start | bytes 2308
  3.5 11.6 %copy-start.6 = (s32[8]{0:T(128)S(1)}, s32[8]{0:T(128)}, u32[]{:S(2)}) copy-start(s32[8]{0:T(128)} %param.17) | copy-start | bytes 100
  3.5 11.6 %copy-start.7 = (s32[8]{0:T(128)S(1)}, s32[8]{0:T(128)}, u32[]{:S(2)}) copy-start(s32[8]{0:T(128)} %param.18) | copy-start | bytes 100
  3.5 33.0 %copy-start = (s32[8,64,64]{2,1,0:T(8,128)S(1)}, s32[8,64,64]{2,1,0:T(8,128)}, u32[]{:S(2)}) copy-start(s32[8,64,64]{2,1,0:T(8,128)} %mask_ref.1) | copy-start | bytes 393220
  3.6 33.0 %all-to-all-start = ((bf16[128,40,128]{2,1,0:T(8,128)(2,1)}), bf16[128,40,128]{2,1,0:T(8,128)(2,1)S(1)}, u32[]{:S(2)}, u32[]{:S(2)}) async-start(bf16[128,40,128]{2,1,0:T(8,128)(2,1)} %bitcast.3), calls=%async_computation | async-start | bytes 2621440 | tf_op jit(solution)/shard_map/all_to_all | solution.py:451
  96.3 26.6 %all-to-all-start.1 = ((bf16[128,40,128]{2,1,0:T(8,128)(2,1)}), bf16[128,40,128]{2,1,0:T(8,128)(2,1)S(1)}, u32[]{:S(2)}, u32[]{:S(2)}) async-start(bf16[128,40,128]{2,1,0:T(8,128)(2,1)} %attend.1), calls=%async_computation.1 | async-start | bytes 2621440 | tf_op jit(solution)/shard_map/all_to_all | solution.py:458

commit v4 on v3

--- a/solution.py
+++ b/solution.py
@@ -11,6 +11,7 @@
 NEG = -1e30
 LOG2E = 1.4426950408889634
 HUGE = 2.0**100
+TINY = 2.0**-120
 STEP = 16
 TAIL = 4
 CHUNK = 64
@@ -25,14 +26,23 @@
     return jnp.concatenate([jnp.where(col < x, 0.0, NEG) for x in lims], 1)
 
 
-def pack_kernel(dims, q_ref, tk_ref, tv_ref, o_ref, block, sems):
+def pack_kernel(dims, q_hbm, tk_hbm, tv_hbm, o_ref, q_ref, tk_ref, tv_ref, block, sems):
     heads, splits, tl, group, hd = dims
-    tk = tk_ref[0].astype(F32)
-    tv = tv_ref[0].astype(F32)
+    pairs = ((q_hbm, q_ref), (tk_hbm, tk_ref), (tv_hbm, tv_ref))
+    arrivals = [
+        pltpu.make_async_copy(src.at[0], dst, sems.at[splits + t])
+        for t, (src, dst) in enumerate(pairs)
+    ]
+    for c in arrivals:
+        c.start()
+    for c in arrivals:
+        c.wait()
+    tk = tk_ref[...].astype(F32)
+    tv = tv_ref[...].astype(F32)
     for h in range(heads):
         for i in range(tl):
             block[h, i * group : (i + 1) * group, :] = q_ref[
-                0, i, h * group : (h + 1) * group, :
+                i, h * group : (h + 1) * group, :
             ]
         both = [t[i, h : h + 1] for t in (tk, tv) for i in range(tl)]
         block[h, tl * group :, :] = jnp.concatenate(both, 0).astype(BF16)
@@ -48,15 +58,18 @@
 def pack(queries, tree_keys, tree_values, dims):
     heads, splits, tl, group, hd = dims
     rows = tl * group + 2 * tl
-    vmem = pl.BlockSpec(memory_space=pltpu.VMEM)
+    hbm = pl.BlockSpec(memory_space=pltpu.HBM)
     return pl.pallas_call(
         functools.partial(pack_kernel, dims),
         out_shape=jax.ShapeDtypeStruct((heads, splits, rows, hd), BF16),
-        in_specs=[vmem, vmem, vmem],
-        out_specs=pl.BlockSpec(memory_space=pltpu.HBM),
+        in_specs=[hbm, hbm, hbm],
+        out_specs=hbm,
         scratch_shapes=[
+            pltpu.VMEM((tl, heads * group, hd), BF16),
+            pltpu.VMEM((tl, heads, hd), BF16),
+            pltpu.VMEM((tl, heads, hd), BF16),
             pltpu.VMEM((heads, rows, hd), BF16),
-            pltpu.SemaphoreType.DMA((splits,)),
+            pltpu.SemaphoreType.DMA((splits + 3,)),
         ],
         compiler_params=pltpu.CompilerParams(vmem_limit_bytes=8 * 2**20),
         name="pack",
@@ -136,6 +149,7 @@
     mask_ref,
     k_hbm,
     v_hbm,
+    o_hbm,
     o_ref,
     k_ref,
     v_ref,
@@ -144,6 +158,7 @@
     acc,
     top,
     sems,
+    out_sems,
 ):
     requests, splits, tl, group, pages, page, hd = dims
     rows = tl * group
@@ -247,18 +262,21 @@
         blocks = count // rows
         total = jnp.sum(l_s[0:count, :], 1, keepdims=True)
         total = jnp.broadcast_to(total, (count, hd))
-        some = total > 0.0
-        safe = jnp.where(some, total, 1.0)
-        o = (acc[0:count, :] / safe).astype(BF16)
+        o = (acc[0:count, :] / jnp.maximum(total, TINY)).astype(BF16)
         o_ref[pl.ds(r * splits, blocks), 0:rows, :] = o.reshape(blocks, rows, hd)
-        shift = m_s[pl.ds(r * full_rows, count), :]
-        lse = jnp.where(some, shift + jnp.log2(safe), NEG)
-        lse = lse.reshape(blocks, tl, group, hd)
         lane = lax.broadcasted_iota(jnp.int32, (1, 1, hd), 2)
         span = hd // tl
-        both = lse[:, tl - 1]
-        for i in range(tl - 2, -1, -1):
-            both = jnp.where(lane < (i + 1) * span, lse[:, i], both)
+
+        def by_lane(x):
+            x = x.reshape(blocks, tl, group, hd)
+            out = x[:, tl - 1]
+            for i in range(tl - 2, -1, -1):
+                out = jnp.where(lane < (i + 1) * span, x[:, i], out)
+            return out
+
+        sums = by_lane(total)
+        shift = by_lane(m_s[pl.ds(r * full_rows, count), :])
+        both = jnp.where(sums > 0.0, shift + jnp.log2(jnp.maximum(sums, TINY)), NEG)
         high = both.astype(BF16).astype(F32)
         mid = (both - high).astype(BF16).astype(F32)
         low = both - high - mid
@@ -278,6 +296,10 @@
                 at = pl.multiple_of(block * rows + i * group, group)
                 m_s[pl.ds(at, group), :] = jnp.broadcast_to(s, (group, hd))
 
+    def send(r):
+        at = pl.ds(r * splits, splits)
+        return pltpu.make_async_copy(o_ref.at[at], o_hbm.at[at], out_sems.at[r])
+
     def rows_of(r, first, count):
         return pl.ds(pl.multiple_of(r * full_rows + first, 8), count)
 
@@ -352,11 +374,18 @@
             def _():
                 request(r, c * CHUNK)
 
+        send(r).start()
+
+    for r in range(requests):
+        send(r).wait()
+
     @pl.when(jnp.logical_not(jnp.max(top[...]) < HUGE))
     def _():
         @pl.loop(0, requests)
         def _(r):
             request_online(r)
+            send(r).start()
+            send(r).wait()
 
 
 def attend(lists, x, mask, key_cache, value_cache, dims):
@@ -369,8 +398,9 @@
         functools.partial(attn_kernel, dims),
         out_shape=jax.ShapeDtypeStruct(x.shape, BF16),
         in_specs=[smem, vmem, vmem, hbm, hbm],
-        out_specs=vmem,
+        out_specs=hbm,
         scratch_shapes=[
+            pltpu.VMEM(x.shape, BF16),
             pltpu.VMEM((pages, page, hd), BF16),
             pltpu.VMEM((pages, page, hd), BF16),
             pltpu.VMEM((requests * full_rows, hd), F32),
@@ -378,6 +408,7 @@
             pltpu.VMEM((full_rows, hd), F32),
             pltpu.VMEM((8, hd), F32),
             pltpu.SemaphoreType.DMA((2, requests)),
+            pltpu.SemaphoreType.DMA((requests,)),
         ],
         compiler_params=pltpu.CompilerParams(vmem_limit_bytes=48 * 2**20),
         name="attend",

time: 127 us -> 132 us (1.039); the launches traced: 125 us -> 132 us
  Pallas kernels: 71.7 us -> 79.3 us
    pallas_call x1, Pallas kernels: 59.7 us -> 67.2 us  [attend(): pl.pallas_call(functools.partial(attn_kernel, dims), out_shape=jax.ShapeD...]
where the time goes in v4:
time: 132 us
  Pallas kernels  79.3 us (60%)
  waiting for transfers between devices  32.9 us (25%)
  starting transfers between devices  16.3 us (12%)
  local copies, waits for them, and re-layouts  2.99 us (2%)
    pallas_call x1, Pallas kernels, attend(): pl.pallas_call(functools.partial(attn_kernel, dims), out_shape=jax.ShapeD...  67.2 us
    all_to_all x1, waiting for transfers between devices, per_device(): y = lax.all_to_all(y, BOTH, 0, 0, tiled=True)  20.3 us
    all_to_all x1, waiting for transfers between devices, per_device(): x = lax.all_to_all(x, BOTH, 0, 0, tiled=True)  12.6 us
    all_to_all x1, starting transfers between devices, per_device(): x = lax.all_to_all(x, BOTH, 0, 0, tiled=True)  11.5 us
    pallas_call x1, Pallas kernels, prepare(): pl.pallas_call(functools.partial(prepare_kernel, dims), out_shape=jax.Sha...  8.78 us
    all_to_all x1, starting transfers between devices, per_device(): y = lax.all_to_all(y, BOTH, 0, 0, tiled=True)  4.77 us
  transfers between devices with their start and end apart: 2, of which 2 were waited for; matrix products, arithmetic and copies ran while one was open for 1% of the time, Pallas kernels for 7%

profile of v4, /device:TPU:1, one launch (start us, length us, event | category | flops | bytes accessed | tf_op | source)
XLA Modules:
  0.0 132.3 jit_solution(1778760790884441438)
XLA Ops:
  0.0 0.0 copy-start.1
  0.0 0.8 copy-done.1
  0.8 0.0 copy-start.2
  0.8 0.7 copy-done.2
  1.5 0.0 copy-start.3
  1.5 0.7 copy-done.3
  2.2 1.4 %pack.1 = bf16[8,16,40,128]{3,2,1,0:T(8,128)(2,1)} custom-call(bf16[1,4,64,128]{3,2,1,0:T(8,128)(2,1)S(1)} %copy-done.1, bf16[1,4,8,128]{3,2,1,0:T(8,128)(2,1)S(1)} %copy-done.2, bf16[1,4,8,128]{3,2,1,0:T(8,128)(2,1)S(1)} %copy-done.3), custom_call_target="tpu_custom_call" | custom-call | tf_op jit(solution)/shard_map/pack/pallas_call | solution.py:62
  3.6 0.0 copy-start.4
  3.6 0.0 copy-start.5
  3.6 0.0 copy-start.6
  3.6 0.0 copy-start.7
  3.6 0.0 copy-start
  3.7 11.5 %all-to-all-start = ((bf16[128,40,128]{2,1,0:T(8,128)(2,1)}), bf16[128,40,128]{2,1,0:T(8,128)(2,1)S(1)}, u32[]{:S(2)}, u32[]{:S(2)}) async-start(bf16[128,40,128]{2,1,0:T(8,128)(2,1)} %bitcast.3), calls=%async_computation | async-start | bytes 2621440 | tf_op jit(solution)/shard_map/all_to_all | solution.py:482
  15.2 0.0 copy-done.4
  15.2 0.0 copy-done.5
  15.2 0.0 copy-done.6
  15.2 0.0 copy-done.7
  15.2 0.1 concatenate.3.meta
  15.3 8.8 %prepare.1.lists = s32[226]{0:T(256)S(1)} custom-call(s32[401]{0:T(512)S(1)} %concatenate.3.meta), custom_call_target="tpu_custom_call" | custom-call | bytes 16777216 | tf_op jit(solution)/shard_map/prepare/pallas_call | solution.py:132
  24.1 12.6 %all-to-all-done.x_ref = bf16[128,40,128]{2,1,0:T(8,128)(2,1)S(1)} async-done(((bf16[128,40,128]{2,1,0:T(8,128)(2,1)}), bf16[128,40,128]{2,1,0:T(8,128)(2,1)S(1)}, u32[]{:S(2)}, u32[]{:S(2)}) %all-to-all-start) | async-done | bytes 1310752 | tf_op jit(solution)/shard_map/all_to_all | solution.py:482
  36.7 0.0 copy-done
  36.7 67.2 %attend.1 = bf16[128,40,128]{2,1,0:T(8,128)(2,1)} custom-call(s32[226]{0:T(256)S(1)} %prepare.1.lists, bf16[128,40,128]{2,1,0:T(8,128)(2,1)S(1)} %all-to-all-done.x_ref, s32[8,64,64]{2,1,0:T(8,128)S(1)} %copy-done, bf16[1,192,128,128]{3,2,1,0:T(8,128)(2,1)} %k_hbm.1, bf16[1,192,128,128]{3,2,1,0:T(8,128)(2,1)} %v_hbm.1), custom_call_target="tpu_custom_call" | custom-call | tf_op jit(solution)/shard_map/attend/pallas_call | solution.py:397
  103.9 4.8 %all-to-all-start.1 = ((bf16[128,40,128]{2,1,0:T(8,128)(2,1)}), bf16[128,40,128]{2,1,0:T(8,128)(2,1)S(1)}, u32[]{:S(2)}, u32[]{:S(2)}) async-start(bf16[128,40,128]{2,1,0:T(8,128)(2,1)} %attend.1), calls=%async_computation.1 | async-start | bytes 2621440 | tf_op jit(solution)/shard_map/all_to_all | solution.py:489
  108.7 0.6 dynamic-slice.2
  110.0 0.1 pad_add_fusion.where_ref
  110.1 20.3 %all-to-all-done.1.y_ref = bf16[128,40,128]{2,1,0:T(8,128)(2,1)S(1)} async-done(((bf16[128,40,128]{2,1,0:T(8,128)(2,1)}), bf16[128,40,128]{2,1,0:T(8,128)(2,1)S(1)}, u32[]{:S(2)}, u32[]{:S(2)}) %all-to-all-start.1) | async-done | bytes 1310752 | tf_op jit(solution)/shard_map/all_to_all | solution.py:489
  130.4 1.9 %join.1 = bf16[1,4,64,128]{3,2,1,0:T(8,128)(2,1)} custom-call(s32[2]{0:T(128)S(1)} %pad_add_fusion.where_ref, bf16[128,40,128]{2,1,0:T(8,128)(2,1)S(1)} %all-to-all-done.1.y_ref), custom_call_target="tpu_custom_call" | custom-call | tf_op jit(solution)/shard_map/join/pallas_call | solution.py:447
Async XLA Ops:
  0.0 0.8 copy-start.1
  0.8 0.7 copy-start.2
  1.5 0.7 copy-start.3
  3.6 11.6 %copy-start.4 = (s32[192]{0:T(256)S(1)}, s32[192]{0:T(256)}, u32[]{:S(2)}) copy-start(s32[192]{0:T(256)} %param.15) | copy-start | bytes 2308
  3.6 11.6 %copy-start.5 = (s32[192]{0:T(256)S(1)}, s32[192]{0:T(256)}, u32[]{:S(2)}) copy-start(s32[192]{0:T(256)} %param.16) | copy-start | bytes 2308
  3.6 11.6 %copy-start.6 = (s32[8]{0:T(128)S(1)}, s32[8]{0:T(128)}, u32[]{:S(2)}) copy-start(s32[8]{0:T(128)} %param.17) | copy-start | bytes 100
  3.6 11.6 %copy-start.7 = (s32[8]{0:T(128)S(1)}, s32[8]{0:T(128)}, u32[]{:S(2)}) copy-start(s32[8]{0:T(128)} %param.18) | copy-start | bytes 100
  3.6 33.0 %copy-start = (s32[8,64,64]{2,1,0:T(8,128)S(1)}, s32[8,64,64]{2,1,0:T(8,128)}, u32[]{:S(2)}) copy-start(s32[8,64,64]{2,1,0:T(8,128)} %mask_ref.1) | copy-start | bytes 393220
  3.7 33.0 %all-to-all-start = ((bf16[128,40,128]{2,1,0:T(8,128)(2,1)}), bf16[128,40,128]{2,1,0:T(8,128)(2,1)S(1)}, u32[]{:S(2)}, u32[]{:S(2)}) async-start(bf16[128,40,128]{2,1,0:T(8,128)(2,1)} %bitcast.3), calls=%async_computation | async-start | bytes 2621440 | tf_op jit(solution)/shard_map/all_to_all | solution.py:482
  103.9 26.4 %all-to-all-start.1 = ((bf16[128,40,128]{2,1,0:T(8,128)(2,1)}), bf16[128,40,128]{2,1,0:T(8,128)(2,1)S(1)}, u32[]{:S(2)}, u32[]{:S(2)}) async-start(bf16[128,40,128]{2,1,0:T(8,128)(2,1)} %attend.1), calls=%async_computation.1 | async-start | bytes 2621440 | tf_op jit(solution)/shard_map/all_to_all | solution.py:489

commit v5 on v4

--- a/solution.py
+++ b/solution.py
@@ -71,7 +71,6 @@
             pltpu.VMEM((heads, rows, hd), BF16),
             pltpu.SemaphoreType.DMA((splits + 3,)),
         ],
-        compiler_params=pltpu.CompilerParams(vmem_limit_bytes=8 * 2**20),
         name="pack",
     )(queries, tree_keys, tree_values)
 

time: 132 us -> 130 us (0.985); the launches traced: 132 us -> 128 us
  Pallas kernels: 79.3 us -> 71.7 us
  starting transfers between devices: 16.3 us -> 21.8 us
  local copies, waits for them, and re-layouts: 2.99 us -> 0.77 us
    pallas_call x1, Pallas kernels: 67.2 us -> 58.9 us  [attend(): pl.pallas_call(functools.partial(attn_kernel, dims), out_shape=jax.ShapeD...]
    all_to_all x1, starting transfers between devices: 4.77 us -> 10.3 us  [per_device(): y = lax.all_to_all(y, BOTH, 0, 0, tiled=True)]
    unnamed x16 -> x10, local copies, waits for them, and re-layouts: 2.26 us -> 0.03 us
where the time goes in v5:
time: 130 us; the launch traced here: 128 us
  Pallas kernels  71.7 us (55%)
  waiting for transfers between devices  32.7 us (25%)
  starting transfers between devices  21.8 us (17%)
    pallas_call x1, Pallas kernels, attend(): pl.pallas_call(functools.partial(attn_kernel, dims), out_shape=jax.ShapeD...  58.9 us
    all_to_all x1, waiting for transfers between devices, per_device(): y = lax.all_to_all(y, BOTH, 0, 0, tiled=True)  20.1 us
    all_to_all x1, waiting for transfers between devices, per_device(): x = lax.all_to_all(x, BOTH, 0, 0, tiled=True)  12.6 us
    all_to_all x1, starting transfers between devices, per_device(): x = lax.all_to_all(x, BOTH, 0, 0, tiled=True)  11.5 us
    all_to_all x1, starting transfers between devices, per_device(): y = lax.all_to_all(y, BOTH, 0, 0, tiled=True)  10.3 us
    pallas_call x1, Pallas kernels, prepare(): pl.pallas_call(functools.partial(prepare_kernel, dims), out_shape=jax.Sha...  8.78 us
  transfers between devices with their start and end apart: 2, of which 2 were waited for; matrix products, arithmetic and copies ran while one was open for 1% of the time, Pallas kernels for 7%

profile of v5, /device:TPU:1, one launch (start us, length us, event | category | flops | bytes accessed | tf_op | source)
XLA Modules:
  0.0 127.8 jit_solution(14129215880498694116)
XLA Ops:
  0.0 2.1 %pack.1 = bf16[8,16,40,128]{3,2,1,0:T(8,128)(2,1)} custom-call(bf16[1,4,64,128]{3,2,1,0:T(8,128)(2,1)} %q_hbm.1, bf16[1,4,8,128]{3,2,1,0:T(8,128)(2,1)} %tk_hbm.1, bf16[1,4,8,128]{3,2,1,0:T(8,128)(2,1)} %tv_hbm.1), custom_call_target="tpu_custom_call" | custom-call | tf_op jit(solution)/shard_map/pack/pallas_call | solution.py:62
  2.1 0.0 copy-start.1
  2.1 0.0 copy-start.2
  2.1 0.0 copy-start.3
  2.2 0.0 copy-start.4
  2.2 0.0 copy-start
  2.2 11.5 %all-to-all-start = ((bf16[128,40,128]{2,1,0:T(8,128)(2,1)}), bf16[128,40,128]{2,1,0:T(8,128)(2,1)S(1)}, u32[]{:S(2)}, u32[]{:S(2)}) async-start(bf16[128,40,128]{2,1,0:T(8,128)(2,1)} %bitcast.4), calls=%async_computation | async-start | bytes 2621440 | tf_op jit(solution)/shard_map/all_to_all | solution.py:481
  13.7 0.0 copy-done.1
  13.7 0.0 copy-done.2
  13.7 0.0 copy-done.3
  13.7 0.0 copy-done.4
  13.7 0.1 concatenate.3.meta
  13.8 8.8 %prepare.1.lists = s32[226]{0:T(256)S(1)} custom-call(s32[401]{0:T(512)S(1)} %concatenate.3.meta), custom_call_target="tpu_custom_call" | custom-call | bytes 16777216 | tf_op jit(solution)/shard_map/prepare/pallas_call | solution.py:131
  22.6 12.6 %all-to-all-done.x_ref = bf16[128,40,128]{2,1,0:T(8,128)(2,1)S(1)} async-done(((bf16[128,40,128]{2,1,0:T(8,128)(2,1)}), bf16[128,40,128]{2,1,0:T(8,128)(2,1)S(1)}, u32[]{:S(2)}, u32[]{:S(2)}) %all-to-all-start) | async-done | bytes 1310752 | tf_op jit(solution)/shard_map/all_to_all | solution.py:481
  35.2 0.0 copy-done
  35.2 58.9 %attend.1 = bf16[128,40,128]{2,1,0:T(8,128)(2,1)} custom-call(s32[226]{0:T(256)S(1)} %prepare.1.lists, bf16[128,40,128]{2,1,0:T(8,128)(2,1)S(1)} %all-to-all-done.x_ref, s32[8,64,64]{2,1,0:T(8,128)S(1)} %copy-done, bf16[1,192,128,128]{3,2,1,0:T(8,128)(2,1)} %k_hbm.1, bf16[1,192,128,128]{3,2,1,0:T(8,128)(2,1)} %v_hbm.1), custom_call_target="tpu_custom_call" | custom-call | tf_op jit(solution)/shard_map/attend/pallas_call | solution.py:396
  94.1 10.3 %all-to-all-start.1 = ((bf16[128,40,128]{2,1,0:T(8,128)(2,1)}), bf16[128,40,128]{2,1,0:T(8,128)(2,1)S(1)}, u32[]{:S(2)}, u32[]{:S(2)}) async-start(bf16[128,40,128]{2,1,0:T(8,128)(2,1)} %attend.1), calls=%async_computation.1 | async-start | bytes 2621440 | tf_op jit(solution)/shard_map/all_to_all | solution.py:488
  104.4 0.7 dynamic-slice.2
  105.7 0.1 pad_add_fusion.where_ref
  105.7 20.1 %all-to-all-done.1.y_ref = bf16[128,40,128]{2,1,0:T(8,128)(2,1)S(1)} async-done(((bf16[128,40,128]{2,1,0:T(8,128)(2,1)}), bf16[128,40,128]{2,1,0:T(8,128)(2,1)S(1)}, u32[]{:S(2)}, u32[]{:S(2)}) %all-to-all-start.1) | async-done | bytes 1310752 | tf_op jit(solution)/shard_map/all_to_all | solution.py:488
  125.9 1.9 %join.1 = bf16[1,4,64,128]{3,2,1,0:T(8,128)(2,1)} custom-call(s32[2]{0:T(128)S(1)} %pad_add_fusion.where_ref, bf16[128,40,128]{2,1,0:T(8,128)(2,1)S(1)} %all-to-all-done.1.y_ref), custom_call_target="tpu_custom_call" | custom-call | tf_op jit(solution)/shard_map/join/pallas_call | solution.py:446
Async XLA Ops:
  2.1 11.6 %copy-start.1 = (s32[192]{0:T(256)S(1)}, s32[192]{0:T(256)}, u32[]{:S(2)}) copy-start(s32[192]{0:T(256)} %param.15) | copy-start | bytes 2308
  2.1 11.6 %copy-start.2 = (s32[192]{0:T(256)S(1)}, s32[192]{0:T(256)}, u32[]{:S(2)}) copy-start(s32[192]{0:T(256)} %param.16) | copy-start | bytes 2308
  2.1 11.6 %copy-start.3 = (s32[8]{0:T(128)S(1)}, s32[8]{0:T(128)}, u32[]{:S(2)}) copy-start(s32[8]{0:T(128)} %param.17) | copy-start | bytes 100
  2.2 11.6 %copy-start.4 = (s32[8]{0:T(128)S(1)}, s32[8]{0:T(128)}, u32[]{:S(2)}) copy-start(s32[8]{0:T(128)} %param.18) | copy-start | bytes 100
  2.2 33.0 %copy-start = (s32[8,64,64]{2,1,0:T(8,128)S(1)}, s32[8,64,64]{2,1,0:T(8,128)}, u32[]{:S(2)}) copy-start(s32[8,64,64]{2,1,0:T(8,128)} %mask_ref.1) | copy-start | bytes 393220
  2.2 33.0 %all-to-all-start = ((bf16[128,40,128]{2,1,0:T(8,128)(2,1)}), bf16[128,40,128]{2,1,0:T(8,128)(2,1)S(1)}, u32[]{:S(2)}, u32[]{:S(2)}) async-start(bf16[128,40,128]{2,1,0:T(8,128)(2,1)} %bitcast.4), calls=%async_computation | async-start | bytes 2621440 | tf_op jit(solution)/shard_map/all_to_all | solution.py:481
  94.1 31.8 %all-to-all-start.1 = ((bf16[128,40,128]{2,1,0:T(8,128)(2,1)}), bf16[128,40,128]{2,1,0:T(8,128)(2,1)S(1)}, u32[]{:S(2)}, u32[]{:S(2)}) async-start(bf16[128,40,128]{2,1,0:T(8,128)(2,1)} %attend.1), calls=%async_computation.1 | async-start | bytes 2621440 | tf_op jit(solution)/shard_map/all_to_all | solution.py:488

commit v6 on v5

--- a/solution.py
+++ b/solution.py
@@ -331,9 +331,15 @@
 
             @pl.when(quarters == c)
             def _(c=c):
-                k, v, bias = last_block(r, start, c * TAIL)
+                k, v, bias = last_block(r, start + (c - 1) * TAIL, TAIL)
+                if c > 1:
+                    k0, v0 = whole_block(r, start, (c - 1) * TAIL)
+                    k, v = jnp.concatenate([k0, k], 0), jnp.concatenate([v0, v], 0)
                 s = lax.dot_general(q, k, NT, preferred_element_type=F32)
-                add(at, where, s + bias, v)
+                edge = (c - 1) * TAIL * page
+                last = s[:, edge:] + bias
+                s = jnp.concatenate([s[:, :edge], last], 1) if c > 1 else last
+                add(at, where, s, v)
 
         total = finish(r, count)
         high = functools.reduce(

time: 130 us -> 128 us (0.985); the launches traced: 128 us -> 128 us
  Pallas kernels: 71.7 us -> 74.9 us
  starting transfers between devices: 21.8 us -> 18.8 us
    pallas_call x1, Pallas kernels: 58.9 us -> 62.1 us  [attend(): pl.pallas_call(functools.partial(attn_kernel, dims), out_shape=jax.ShapeD...]
    all_to_all x1, starting transfers between devices: 10.3 us -> 7.27 us  [per_device(): y = lax.all_to_all(y, BOTH, 0, 0, tiled=True)]
where the time goes in v6:
time: 128 us
  Pallas kernels  74.9 us (59%)
  waiting for transfers between devices  32.7 us (26%)
  starting transfers between devices  18.8 us (15%)
    pallas_call x1, Pallas kernels, attend(): pl.pallas_call(functools.partial(attn_kernel, dims), out_shape=jax.ShapeD...  62.1 us
    all_to_all x1, waiting for transfers between devices, per_device(): y = lax.all_to_all(y, BOTH, 0, 0, tiled=True)  20.1 us
    all_to_all x1, waiting for transfers between devices, per_device(): x = lax.all_to_all(x, BOTH, 0, 0, tiled=True)  12.6 us
    all_to_all x1, starting transfers between devices, per_device(): x = lax.all_to_all(x, BOTH, 0, 0, tiled=True)  11.5 us
    pallas_call x1, Pallas kernels, prepare(): pl.pallas_call(functools.partial(prepare_kernel, dims), out_shape=jax.Sha...  8.78 us
    all_to_all x1, starting transfers between devices, per_device(): y = lax.all_to_all(y, BOTH, 0, 0, tiled=True)  7.27 us
  transfers between devices with their start and end apart: 2, of which 2 were waited for; matrix products, arithmetic and copies ran while one was open for 1% of the time, Pallas kernels for 7%

profile of v6, /device:TPU:1, one launch (start us, length us, event | category | flops | bytes accessed | tf_op | source)
XLA Modules:
  0.0 128.0 jit_solution(12594539040101663692)
XLA Ops:
  0.0 2.1 %pack.1 = bf16[8,16,40,128]{3,2,1,0:T(8,128)(2,1)} custom-call(bf16[1,4,64,128]{3,2,1,0:T(8,128)(2,1)} %q_hbm.1, bf16[1,4,8,128]{3,2,1,0:T(8,128)(2,1)} %tk_hbm.1, bf16[1,4,8,128]{3,2,1,0:T(8,128)(2,1)} %tv_hbm.1), custom_call_target="tpu_custom_call" | custom-call | tf_op jit(solution)/shard_map/pack/pallas_call | solution.py:62
  2.1 0.0 copy-start.1
  2.1 0.0 copy-start.2
  2.1 0.0 copy-start.3
  2.2 0.0 copy-start.4
  2.2 0.0 copy-start
  2.2 11.5 %all-to-all-start = ((bf16[128,40,128]{2,1,0:T(8,128)(2,1)}), bf16[128,40,128]{2,1,0:T(8,128)(2,1)S(1)}, u32[]{:S(2)}, u32[]{:S(2)}) async-start(bf16[128,40,128]{2,1,0:T(8,128)(2,1)} %bitcast.4), calls=%async_computation | async-start | bytes 2621440 | tf_op jit(solution)/shard_map/all_to_all | solution.py:487
  13.7 0.0 copy-done.1
  13.7 0.0 copy-done.2
  13.7 0.0 copy-done.3
  13.7 0.0 copy-done.4
  13.7 0.1 concatenate.3.meta
  13.8 8.8 %prepare.1.lists = s32[226]{0:T(256)S(1)} custom-call(s32[401]{0:T(512)S(1)} %concatenate.3.meta), custom_call_target="tpu_custom_call" | custom-call | bytes 16777216 | tf_op jit(solution)/shard_map/prepare/pallas_call | solution.py:131
  22.6 12.6 %all-to-all-done.x_ref = bf16[128,40,128]{2,1,0:T(8,128)(2,1)S(1)} async-done(((bf16[128,40,128]{2,1,0:T(8,128)(2,1)}), bf16[128,40,128]{2,1,0:T(8,128)(2,1)S(1)}, u32[]{:S(2)}, u32[]{:S(2)}) %all-to-all-start) | async-done | bytes 1310752 | tf_op jit(solution)/shard_map/all_to_all | solution.py:487
  35.2 0.0 copy-done
  35.2 62.1 %attend.1 = bf16[128,40,128]{2,1,0:T(8,128)(2,1)} custom-call(s32[226]{0:T(256)S(1)} %prepare.1.lists, bf16[128,40,128]{2,1,0:T(8,128)(2,1)S(1)} %all-to-all-done.x_ref, s32[8,64,64]{2,1,0:T(8,128)S(1)} %copy-done, bf16[1,192,128,128]{3,2,1,0:T(8,128)(2,1)} %k_hbm.1, bf16[1,192,128,128]{3,2,1,0:T(8,128)(2,1)} %v_hbm.1), custom_call_target="tpu_custom_call" | custom-call | tf_op jit(solution)/shard_map/attend/pallas_call | solution.py:402
  97.3 7.3 %all-to-all-start.1 = ((bf16[128,40,128]{2,1,0:T(8,128)(2,1)}), bf16[128,40,128]{2,1,0:T(8,128)(2,1)S(1)}, u32[]{:S(2)}, u32[]{:S(2)}) async-start(bf16[128,40,128]{2,1,0:T(8,128)(2,1)} %attend.1), calls=%async_computation.1 | async-start | bytes 2621440 | tf_op jit(solution)/shard_map/all_to_all | solution.py:494
  104.6 0.7 dynamic-slice.2
  105.9 0.1 pad_add_fusion.where_ref
  105.9 20.1 %all-to-all-done.1.y_ref = bf16[128,40,128]{2,1,0:T(8,128)(2,1)S(1)} async-done(((bf16[128,40,128]{2,1,0:T(8,128)(2,1)}), bf16[128,40,128]{2,1,0:T(8,128)(2,1)S(1)}, u32[]{:S(2)}, u32[]{:S(2)}) %all-to-all-start.1) | async-done | bytes 1310752 | tf_op jit(solution)/shard_map/all_to_all | solution.py:494
  126.1 1.9 %join.1 = bf16[1,4,64,128]{3,2,1,0:T(8,128)(2,1)} custom-call(s32[2]{0:T(128)S(1)} %pad_add_fusion.where_ref, bf16[128,40,128]{2,1,0:T(8,128)(2,1)S(1)} %all-to-all-done.1.y_ref), custom_call_target="tpu_custom_call" | custom-call | tf_op jit(solution)/shard_map/join/pallas_call | solution.py:452
Async XLA Ops:
  2.1 11.6 %copy-start.1 = (s32[192]{0:T(256)S(1)}, s32[192]{0:T(256)}, u32[]{:S(2)}) copy-start(s32[192]{0:T(256)} %param.15) | copy-start | bytes 2308
  2.1 11.6 %copy-start.2 = (s32[192]{0:T(256)S(1)}, s32[192]{0:T(256)}, u32[]{:S(2)}) copy-start(s32[192]{0:T(256)} %param.16) | copy-start | bytes 2308
  2.1 11.6 %copy-start.3 = (s32[8]{0:T(128)S(1)}, s32[8]{0:T(128)}, u32[]{:S(2)}) copy-start(s32[8]{0:T(128)} %param.17) | copy-start | bytes 100
  2.2 11.6 %copy-start.4 = (s32[8]{0:T(128)S(1)}, s32[8]{0:T(128)}, u32[]{:S(2)}) copy-start(s32[8]{0:T(128)} %param.18) | copy-start | bytes 100
  2.2 33.0 %copy-start = (s32[8,64,64]{2,1,0:T(8,128)S(1)}, s32[8,64,64]{2,1,0:T(8,128)}, u32[]{:S(2)}) copy-start(s32[8,64,64]{2,1,0:T(8,128)} %mask_ref.1) | copy-start | bytes 393220
  2.2 33.0 %all-to-all-start = ((bf16[128,40,128]{2,1,0:T(8,128)(2,1)}), bf16[128,40,128]{2,1,0:T(8,128)(2,1)S(1)}, u32[]{:S(2)}, u32[]{:S(2)}) async-start(bf16[128,40,128]{2,1,0:T(8,128)(2,1)} %bitcast.4), calls=%async_computation | async-start | bytes 2621440 | tf_op jit(solution)/shard_map/all_to_all | solution.py:487
  97.3 28.8 %all-to-all-start.1 = ((bf16[128,40,128]{2,1,0:T(8,128)(2,1)}), bf16[128,40,128]{2,1,0:T(8,128)(2,1)S(1)}, u32[]{:S(2)}, u32[]{:S(2)}) async-start(bf16[128,40,128]{2,1,0:T(8,128)(2,1)} %attend.1), calls=%async_computation.1 | async-start | bytes 2621440 | tf_op jit(solution)/shard_map/all_to_all | solution.py:494
